TPU v7x, 32 devices: a whole 2x2x4 slice. The times are simulated.
32 devices in a mesh: gy: 8 (over y, x, core), gx: 4 (over z).
Axes of the slice: x: 2, y: 2, z: 4, core: 2. Of those that a mesh axis runs over, the one named last changes fastest.
Arguments:
- even_half: float32 [32, 128, 1024], P('gx', None, 'gy'), may hold values from -90 to 90
- odd_half: float32 [32, 128, 1024], P('gx', None, 'gy'), may hold values from -90 to 90
- slab_slices: int32 [32], replicated, may hold values from 0 to 31, each once
- shells: int32 [32, 32, 32], replicated, may hold values from 0 to 16, as said below
Outputs:
- filtered: float32 [32, 128, 1024], P(None, 'gy', 'gx')
Inputs may be any that keep to these rules, and one draw needn't show every extreme that they name: `slab_slices`: each slot holds a different z slice. `shells`: the zero frequency is in shell 0 and every shell number occurs.
All inputs are finite; a program needn't handle non-finite values.
Results may differ from a plain program's by a relative error of at most 0.0003.
Values sent between devices are 32-bit elements; how exact they have to be, the bound alone decides.
A program may use at most 192 MiB of HBM per device.

v0:
```python
import math

import jax
import jax.numpy as jnp
from jax import lax
from jax.sharding import PartitionSpec as P

SHELLS = 17


def from_behind(block, axis, distance):
    devices = range(lax.axis_size(axis))
    route = [(i - distance, i) for i in devices if i - distance in devices]
    return lax.ppermute(block, axis, route)


def make_tables():
    indices = jnp.arange(32, dtype=jnp.int32)
    angles = 2.0 * math.pi / 32.0 * (indices[:, None] * indices[None, :] % 32).astype(jnp.float32)
    cosines = jnp.cos(angles)
    sine_table = jnp.sin(angles)
    fwd_real = jnp.stack([cosines, -sine_table])
    fwd_cplx = jnp.stack(
        [jnp.stack([cosines, sine_table], axis=1), jnp.stack([-sine_table, cosines], axis=1)]
    )
    inv_cplx = jnp.stack(
        [jnp.stack([cosines, -sine_table], axis=1), jnp.stack([sine_table, cosines], axis=1)]
    )
    inv_real = jnp.stack([cosines, -sine_table], axis=1)
    taper_window = jnp.sin(math.pi * (indices.astype(jnp.float32) + 0.5) / 32.0)
    return (fwd_real, fwd_cplx, inv_cplx, inv_real, taper_window)


def filter_strip(strip, onehot, tables, col_weight):
    fwd_real, fwd_cplx, inv_cplx, inv_real, taper_window = tables
    halves, depth, height, width_x = strip.shape
    box_cols = width_x // 16 - 1
    blocks = strip.reshape(halves, depth, height, box_cols + 1, 16)
    box_stack = jnp.concatenate([blocks[:, :, :, :-1], blocks[:, :, :, 1:]], axis=4)
    box_stack = box_stack * taper_window[:, None, None] * taper_window * col_weight[:, None]
    highest = lax.Precision.HIGHEST
    spectra = jnp.einsum("pkn,hzybn->hpzykb", fwd_real, box_stack, precision=highest)
    spectra = jnp.einsum("qkpn,hpznxb->hqzkxb", fwd_cplx, spectra, precision=highest)
    spectra = jnp.einsum("qkpn,hpnyxb->hqkyxb", fwd_cplx, spectra, precision=highest)
    spectra = spectra.reshape(halves, 2, depth * height * 32, box_cols)
    cross_power = spectra[0, 0] * spectra[1, 0] + spectra[0, 1] * spectra[1, 1]
    power_even = spectra[0, 0] * spectra[0, 0] + spectra[0, 1] * spectra[0, 1]
    power_odd = spectra[1, 0] * spectra[1, 0] + spectra[1, 1] * spectra[1, 1]
    shell_sums = jnp.einsum(
        "sv,mvb->msb", onehot, jnp.stack([cross_power, power_even, power_odd]), precision=highest
    )
    correlation = shell_sums[0] / jnp.sqrt(shell_sums[1] * shell_sums[2] + 1e-06)
    positive = jnp.maximum(correlation, 0.0)
    weights = 2.0 * positive / (1.0 + positive)
    voxel_weight = jnp.einsum("sv,sb->vb", onehot, weights, precision=highest)
    averaged = (spectra[0] + spectra[1]) * 0.5 * voxel_weight
    averaged = averaged.reshape(2, depth, height, 32, box_cols)
    averaged = jnp.einsum("qnpk,pkyxb->qnyxb", inv_cplx, averaged, precision=highest)
    averaged = jnp.einsum("qnpk,pzkxb->qznxb", inv_cplx, averaged, precision=highest)
    result = jnp.einsum("npk,pzykb->zybn", inv_real, averaged, precision=highest)
    result = result * (1.0 / 32768.0) * taper_window[:, None, None] * taper_window
    padding = jnp.zeros((depth, height, 1, 16), result.dtype)
    merged = jnp.concatenate([result[..., :16], padding], axis=2) + jnp.concatenate(
        [padding, result[..., 16:]], axis=2
    )
    return merged.reshape(depth, height, width_x)


def filter_tile(extended, first_row, col_weight, shells):
    tables = make_tables()
    onehot = (jnp.arange(SHELLS, dtype=jnp.int32)[:, None] == shells.reshape(-1)[None, :]).astype(
        jnp.float32
    )
    box_rows = extended.shape[2] // 16 - 1

    def one_row(row_index):
        row_factor = jnp.where(row_index == 0, first_row, 1.0)
        return filter_strip(extended * row_factor, onehot, tables, col_weight)

    strips = lax.map(one_row, jnp.arange(box_rows, dtype=jnp.int32))
    depth = strips.shape[1]
    width_x = strips.shape[3]
    padding = jnp.zeros((1, depth, 16, width_x), strips.dtype)
    summed = jnp.concatenate([strips[:, :, :16], padding], axis=0) + jnp.concatenate(
        [padding, strips[:, :, 16:]], axis=0
    )
    summed = jnp.transpose(summed, (1, 0, 2, 3))
    return summed.reshape(depth, (box_rows + 1) * 16, width_x)


def on_device(even_half, odd_half, slab_slices, shells):
    halves_pair = jnp.stack([even_half, odd_half])
    tile_pair = lax.all_to_all(
        lax.all_to_all(halves_pair, "gy", split_axis=2, concat_axis=3, tiled=True),
        "gx",
        split_axis=3,
        concat_axis=1,
        tiled=True,
    )
    slot_order = (
        slab_slices[None, :] == jnp.arange(slab_slices.shape[0], dtype=jnp.int32)[:, None]
    ).astype(jnp.float32)
    tile_pair = jnp.einsum("zs,hsyx->hzyx", slot_order, tile_pair, precision=lax.Precision.HIGHEST)
    rows_tile = tile_pair.shape[2]
    cols_tile = tile_pair.shape[3]
    upper_cols = from_behind(tile_pair[:, :, :, :16], "gx", -1)
    extended = jnp.concatenate([tile_pair, upper_cols], axis=3)
    upper_rows = from_behind(extended, "gy", -1)
    extended = jnp.concatenate([extended, upper_rows], axis=2)
    col_weight = jnp.ones((cols_tile // 16,), jnp.float32)
    summed = filter_tile(extended, 1.0, col_weight, shells)
    spill_rows = from_behind(summed[:, rows_tile:, :], "gy", 1)
    summed = jnp.concatenate([summed[:, :16, :] + spill_rows, summed[:, 16:rows_tile, :]], axis=1)
    spill_cols = from_behind(summed[:, :, cols_tile:], "gx", 1)
    filtered = jnp.concatenate([summed[:, :, :16] + spill_cols, summed[:, :, 16:cols_tile]], axis=2)
    return filtered


def solution(mesh):
    in_specs = (P("gx", None, "gy"), P("gx", None, "gy"), P(), P())
    out_specs = P(None, "gy", "gx")
    return jax.shard_map(
        on_device, mesh=mesh, in_specs=in_specs, out_specs=out_specs, check_vma=False
    )
```

profile of v0, /device:TPU:10, one launch (start us, length us, event | category | flops | bytes accessed | tf_op | source)
XLA Modules:
  0.0 510.3 jit_solution(1101573173359661318)
XLA Ops:
  0.0 1.8 copy_bitcast_fusion
  1.9 18.0 %all_to_all.36 = f32[2,8,128,128]{3,1,0,2:T(8,128)S(1)} all-to-all(f32[2,8,128,128]{3,1,0,2:T(8,128)S(1)} %pad_maximum_fusion.2), channel_id=1, replica_groups=mesh['gy'=8,'gx'=4] {'gy'}, dimensions={2} | all-to-all | bytes 2097152 | tf_op jit(solution)/shard_map/all_to_all | solution.py:94
  19.8 5.0 copy.46
  24.9 5.6 %reshape.324 = f32[4,1,65536]{2,1,0:T(1,128)S(1)} reshape(f32[1024,2,8,16]{3,2,1,0:T(8,128)} %bitcast.166) | data formatting | bytes 2097152
  30.5 29.1 %all_to_all.37 = f32[4,1,65536]{2,1,0:T(1,128)S(1)} all-to-all(f32[4,1,65536]{2,1,0:T(1,128)S(1)} %reshape.324), channel_id=1, replica_groups=mesh['gy'=8,'gx'=4] {'gx'}, dimensions={0} | all-to-all | bytes 2097152 | tf_op jit(solution)/shard_map/all_to_all | solution.py:93
  59.6 0.5 broadcast.302
  60.1 3.7 reduce
  63.8 6.2 %reshape.325 = f32[1024,2,8,16]{3,2,1,0:T(8,128)} reshape(f32[4,65536]{1,0:T(4,128)S(1)} %reduce) | data formatting | bytes 2097152
  70.0 5.3 %copy.47 = f32[2,8,16,4,256]{4,3,2,1,0:T(4,128)S(1)} copy(f32[2,8,16,4,256]{2,1,0,4,3:T(8,128)} %bitcast.167) | data formatting | bytes 2097152 | tf_op jit(solution)/shard_map/all_to_all | solution.py:93
  75.2 1.2 convolution_bitcast_fusion.1
  76.5 3.7 collective-permute-start
  80.3 10.7 %collective-permute-done = f32[2,32,16,16]{3,1,2,0:T(8,128)S(1)} collective-permute-done((f32[2,32,16,16]{3,1,2,0:T(8,128)S(1)}, f32[2,32,16,16]{3,1,2,0:T(8,128)S(1)}, u32[]{:S(2)}, u32[]{:S(2)}) %collective-permute-start) | collective-permute-done | bytes 65568 | tf_op jit(solution)/shard_map/ppermute | solution.py:14
  91.0 0.1 pad_maximum_fusion.1
  91.1 2.1 collective-permute-start.1
  93.3 1.2 eq.58
  94.5 0.6 multiply_sine_fusion
  95.3 0.6 maximum_bitcast_fusion.13
  96.0 0.6 fusion.113
  96.6 14.3 %collective-permute-done.1 = f32[2,32,16,272]{3,1,2,0:T(8,128)} collective-permute-done((f32[2,32,16,272]{3,1,2,0:T(8,128)S(1)}, f32[2,32,16,272]{3,1,2,0:T(8,128)}, u32[]{:S(2)}, u32[]{:S(2)}) %collective-permute-start.1) | collective-permute-done | bytes 1114144 | tf_op jit(solution)/shard_map/ppermute | solution.py:14
  111.0 3.4 pad_maximum_fusion
  114.3 6.9 %copy.19 = f32[2,32,32,272]{2,3,1,0:T(8,128)} copy(f32[2,32,32,272]{3,1,2,0:T(8,128)} %pad_maximum_fusion) | data formatting | bytes 4456448 | tf_op jit(solution)/shard_map/concatenate | solution.py:109
  121.2 6.5 %fusion.99 = (f32[2,32,32,16,16]{2,4,3,1,0:T(8,128)S(1)}, f32[2,32,32,16,16]{2,4,3,1,0:T(8,128)S(1)}) fusion(f32[2,32,32,17,16]{2,4,3,1,0:T(8,128)} %bitcast.164), kind=kLoop, calls=%fused_computation.122 | loop fusion | bytes 8388608 | tf_op jit(solution)/shard_map/while/body/eval_jaxpr/slice | solution.py:39
  127.7 30.4 %fusion.13 = f32[2,32,32,16,2,32]{5,2,4,3,1,0:T(8,128)} fusion(f32[2,32,32,16,16]{2,4,3,1,0:T(8,128)S(1)} %get-tuple-element.22, f32[2,32,32,16,16]{2,4,3,1,0:T(8,128)S(1)} %get-tuple-element.21, f32[32]{0:T(128)S(1)} %get-tuple-element.53, f32[1,32,32]{2,1,0:T(8,128)S(1)} %get-tuple-element.49, f32[1,32,32]{2,1,0:T(8,128)S(1)} %get-tuple-element.50), kind=kOutput, calls=%fused_computation.14 | convolution fusion | flops 808454144 | bytes 12591232 | tf_op jit(solution)/shard_map/while/body/eval_jaxpr/pkn,hzybn->hpzykb/dot_general | solution.py:42
  158.1 58.1 %fusion.2 = f32[2,2,32,32,32,16,1]{3,4,1,5,2,0,6:T(8,128)} fusion(f32[2,32,32,16,2,32]{5,2,4,3,1,0:T(8,128)} %fusion.13, f32[2,32,2,32,1,1,1]{3,1,2,0,6,5,4:T(8,128)S(1)} %maximum_bitcast_fusion.12), kind=kOutput, calls=%fused_computation.3 | convolution fusion | flops 1610612736 | bytes 16793600 | tf_op jit(solution)/shard_map/while/body/eval_jaxpr/qkpn,hpznxb->hqzkxb/dot_general | solution.py:43
  216.2 41.4 %copy.35 = f32[2,2,32,32,32,16,1]{2,4,1,6,5,3,0:T(8,128)} copy(f32[2,2,32,32,32,16,1]{3,4,1,5,2,0,6:T(8,128)} %fusion.2) | data formatting | bytes 16777216 | tf_op jit(solution)/shard_map/while/body/eval_jaxpr/qkpn,hpznxb->hqzkxb/transpose | solution.py:43
  257.6 32.8 %convolution_bitcast_fusion = f32[2,2,32,32,32,16]{2,4,1,5,3,0:T(8,128)} fusion(f32[2,2,32,32,32,16,1]{2,4,1,6,5,3,0:T(8,128)} %copy.35, f32[2,32,2,32,1,1,1]{3,1,2,0,6,5,4:T(8,128)S(1)} %copy-done.1), kind=kOutput, calls=%fused_computation.4 | convolution fusion | flops 1610612736 | bytes 16793600 | tf_op jit(solution)/shard_map/while/body/eval_jaxpr/qkpn,hpnyxb->hqkyxb/dot_general | solution.py:44
  290.4 38.7 %copy.23 = f32[2,2,32,32,32,16]{4,3,2,5,1,0:T(8,128)} copy(f32[2,2,32,32,32,16]{2,4,1,5,3,0:T(8,128)} %convolution_bitcast_fusion) | data formatting | bytes 16777216 | tf_op jit(solution)/shard_map/while/body/eval_jaxpr/qkpn,hpnyxb->hqkyxb/transpose | solution.py:44
  329.1 20.9 %reshape.299 = f32[2,2,32768,16]{2,3,1,0:T(8,128)} reshape(f32[2,2,32,32,32,16]{4,3,2,5,1,0:T(8,128)} %copy.23) | data formatting | bytes 16777216 | tf_op jit(solution)/shard_map/while/body/eval_jaxpr/reshape | solution.py:45
  350.0 4.1 add_bitcast_fusion.3
  354.1 3.3 fusion.40
  357.5 1.4 convolution_multiply_fusion
  358.9 4.7 mul.313
  363.6 9.6 %copy.24 = f32[32,32,32,16]{0,2,3,1:T(8,128)} copy(f32[32,32,32,16]{2,1,0,3:T(8,128)} %mul.313) | data formatting | bytes 4194304 | tf_op jit(solution)/shard_map/while/body/eval_jaxpr/mul | solution.py:56
  373.2 47.1 %fusion.25 = f32[2,32,32,32,16,1]{3,1,4,2,0,5:T(8,128)S(1)} fusion(f32[2,2,32,32,32,16]{2,4,1,5,3,0:T(8,128)} %convolution_bitcast_fusion, f32[32,32,32,16]{0,2,3,1:T(8,128)} %copy.24, f32[1,32,2,32]{3,1,2,0:T(8,128)S(1)} %get-tuple-element.46, f32[1,32,2,32]{3,1,2,0:T(8,128)S(1)} %get-tuple-element.41), kind=kOutput, calls=%fused_computation.27 | convolution fusion | flops 807407616 | bytes 14696448 | tf_op jit(solution)/shard_map/while/body/eval_jaxpr/qnpk,pkyxb->qnyxb/dot_general | solution.py:58
  420.4 42.0 %fusion.19 = f32[32,32,16,2,32,1]{4,1,5,3,2,0:T(8,128)S(1)} fusion(f32[2,32,32,32,16,1]{3,1,4,2,0,5:T(8,128)S(1)} %fusion.25, f32[2,32,2,32,1,1]{3,1,2,0,5,4:T(8,128)S(1)} %copy-done), kind=kOutput, calls=%fused_computation.19 | convolution fusion | flops 805306368 | bytes 8404992 | tf_op jit(solution)/shard_map/while/body/eval_jaxpr/qnpk,pzkxb->qznxb/dot_general | solution.py:59
  462.5 11.0 %fusion.21 = f32[32,32,16,32]{1,3,2,0:T(8,128)S(1)} fusion(f32[32]{0:T(128)S(1)} %get-tuple-element.53, f32[32]{0:T(128)S(1)} %copy-done.6, f32[32,32,16,2,32,1]{4,1,5,3,2,0:T(8,128)S(1)} %fusion.19, f32[32,1,32]{2,0,1:T(8,128)S(1)} %copy-done.5, f32[32,1,32]{2,0,1:T(8,128)S(1)} %copy-done.3), kind=kOutput, calls=%fused_computation.23 | convolution fusion | flops 403703808 | bytes 6299904 | tf_op jit(solution)/shard_map/while/body/eval_jaxpr/npk,pzykb->zybn/dot_general | solution.py:60
  473.5 1.2 fusion.100
  474.7 0.7 pad_add_fusion
  475.4 1.4 fusion.101
  476.9 4.0 add_bitcast_fusion
  480.9 5.9 %copy.28 = f32[32,2,16,272]{3,2,1,0:T(8,128)S(1)} copy(f32[32,2,16,272]{2,3,0,1:T(8,128)} %add_bitcast_fusion) | data formatting | bytes 2228224 | tf_op jit(solution)/shard_map/transpose | solution.py:87
  486.9 2.7 collective-permute-start.2
  489.6 10.9 %collective-permute-done.2 = f32[32,16,272]{2,1,0:T(8,128)S(1)} collective-permute-done((f32[32,16,272]{2,1,0:T(8,128)S(1)}, f32[32,16,272]{2,1,0:T(8,128)S(1)}, u32[]{:S(2)}, u32[]{:S(2)}) %collective-permute-start.2) | collective-permute-done | bytes 557088 | tf_op jit(solution)/shard_map/ppermute | solution.py:14
  500.5 0.1 slice_add_fusion.1
  500.6 2.8 collective-permute-start.3
  503.4 0.2 slice.127
  503.6 5.2 %collective-permute-done.3 = f32[32,16,16]{2,1,0:T(8,128)S(1)} collective-permute-done((f32[32,16,16]{2,1,0:T(8,128)S(1)}, f32[32,16,16]{2,1,0:T(8,128)S(1)}, u32[]{:S(2)}, u32[]{:S(2)}) %collective-permute-start.3) | collective-permute-done | bytes 32800 | tf_op jit(solution)/shard_map/ppermute | solution.py:14
  508.9 1.0 pad_maximum_fusion.3
  (26 shorter events, 0.5 us)
Async XLA Ops:
  63.8 11.5 %copy-start.7 = (s32[32]{0:T(128)S(1)}, s32[32]{0:T(128)}, u32[]{:S(2)}) copy-start(s32[32]{0:T(128)} %param.6) | copy-start | bytes 388
  76.5 14.4 %collective-permute-start = (f32[2,32,16,16]{3,1,2,0:T(8,128)S(1)}, f32[2,32,16,16]{3,1,2,0:T(8,128)S(1)}, u32[]{:S(2)}, u32[]{:S(2)}) collective-permute-start(f32[2,32,16,16]{3,1,2,0:T(8,128)S(1)} %slice.107), channel_id=1, source_target_pairs={{1,0},{2,1},{3,2},{5,4},{6,5},{7,6},{9,8},{10,9},{11,10},{13,12},{... | collective-permute-start | bytes 196616 | tf_op jit(solution)/shard_map/ppermute | solution.py:14
  91.1 19.8 %collective-permute-start.1 = (f32[2,32,16,272]{3,1,2,0:T(8,128)S(1)}, f32[2,32,16,272]{3,1,2,0:T(8,128)}, u32[]{:S(2)}, u32[]{:S(2)}) collective-permute-start(f32[2,32,16,272]{3,1,2,0:T(8,128)S(1)} %pad_maximum_fusion.1), channel_id=1, source_target_pairs={{4,0},{8,4},{12,8},{16,12},{20,16},{24,20},{28,24},{5,1},{9,5},{13... | collective-permute-start | bytes 3342344 | tf_op jit(solution)/shard_map/ppermute | solution.py:14
  95.1 26.1 %copy-start.2 = (f32[32,1,32]{2,0,1:T(8,128)}, f32[32,1,32]{2,0,1:T(8,128)S(1)}, u32[]{:S(2)}) copy-start(f32[32,1,32]{2,0,1:T(8,128)S(1)} %fusion.83) | copy-start | bytes 12292
  95.3 25.9 %copy-start.4 = (f32[32,1,32]{2,0,1:T(8,128)}, f32[32,1,32]{2,0,1:T(8,128)S(1)}, u32[]{:S(2)}) copy-start(f32[32,1,32]{2,0,1:T(8,128)S(1)} %get-tuple-element.52) | copy-start | bytes 12292
  216.2 41.4 %copy-start.1 = (f32[2,32,2,32,1,1,1]{3,1,2,0,6,5,4:T(8,128)S(1)}, f32[2,32,2,32,1,1,1]{3,1,2,0,6,5,4:T(8,128)}, u32[]{:S(2)}) copy-start(f32[2,32,2,32,1,1,1]{3,1,2,0,6,5,4:T(8,128)} %maximum_bitcast_fusion.13) | copy-start | bytes 49156
  373.2 47.1 %copy-start = (f32[2,32,2,32,1,1]{3,1,2,0,5,4:T(8,128)S(1)}, f32[2,32,2,32,1,1]{3,1,2,0,5,4:T(8,128)}, u32[]{:S(2)}) copy-start(f32[2,32,2,32,1,1]{3,1,2,0,5,4:T(8,128)} %fusion.113) | copy-start | bytes 49156
  420.4 42.1 %copy-start.3 = (f32[32,1,32]{2,0,1:T(8,128)S(1)}, f32[32,1,32]{2,0,1:T(8,128)}, u32[]{:S(2)}) copy-start(f32[32,1,32]{2,0,1:T(8,128)} %copy-done.2) | copy-start | bytes 12292
  420.4 42.1 %copy-start.5 = (f32[32,1,32]{2,0,1:T(8,128)S(1)}, f32[32,1,32]{2,0,1:T(8,128)}, u32[]{:S(2)}) copy-start(f32[32,1,32]{2,0,1:T(8,128)} %copy-done.4) | copy-start | bytes 12292
  420.4 42.1 %copy-start.6 = (f32[32]{0:T(128)S(1)}, f32[32]{0:T(128)}, u32[]{:S(2)}) copy-start(f32[32]{0:T(128)} %get-tuple-element.54) | copy-start | bytes 388
  486.9 13.6 %collective-permute-start.2 = (f32[32,16,272]{2,1,0:T(8,128)S(1)}, f32[32,16,272]{2,1,0:T(8,128)S(1)}, u32[]{:S(2)}, u32[]{:S(2)}) collective-permute-start(f32[32,16,272]{2,1,0:T(8,128)S(1)} %slice.124), channel_id=1, source_target_pairs={{0,4},{4,8},{8,12},{12,16},{16,20},{20,24},{24,28},{1,5},{5,9},{9,... | collective-permute-start | bytes 1671176 | tf_op jit(solution)/shard_map/ppermute | solution.py:14
  500.6 8.3 %collective-permute-start.3 = (f32[32,16,16]{2,1,0:T(8,128)S(1)}, f32[32,16,16]{2,1,0:T(8,128)S(1)}, u32[]{:S(2)}, u32[]{:S(2)}) collective-permute-start(f32[32,16,16]{2,1,0:T(8,128)S(1)} %slice.126), channel_id=1, source_target_pairs={{0,1},{1,2},{2,3},{4,5},{5,6},{6,7},{8,9},{9,10},{10,11},{12,13},{... | collective-permute-start | bytes 98312 | tf_op jit(solution)/shard_map/ppermute | solution.py:14
where the time goes:
time: 520 us; the launch traced here: 510 us
  matrix products  227 us (44%)
  local copies, waits for them, and re-layouts  163 us (31%)
  blocking collectives  47.1 us (9%)
  waiting for transfers between devices  41.2 us (8%)
  other arithmetic  19.3 us (4%)
  starting transfers between devices  11.3 us (2%)
    dot_general x1, matrix products, filter_strip(): jnp.einsum('qkpn,hpznxb->hqzkxb', fwd_cplx, spectra, precision=highest)  58.1 us
    dot_general x1, matrix products, filter_strip(): jnp.einsum('qnpk,pkyxb->qnyxb', inv_cplx, averaged, precision=highest)  47.1 us
    dot_general x1, matrix products, filter_strip(): jnp.einsum('qnpk,pzkxb->qznxb', inv_cplx, averaged, precision=highest)  42 us
    transpose x1, local copies, waits for them, and re-layouts, filter_strip(): jnp.einsum('qkpn,hpznxb->hqzkxb', fwd_cplx, spectra, precision=highest)  41.4 us
    ppermute x4, waiting for transfers between devices, from_behind(): return lax.ppermute(block, axis, route)  41.2 us
    transpose x1, local copies, waits for them, and re-layouts, filter_strip(): jnp.einsum('qkpn,hpnyxb->hqkyxb', fwd_cplx, spectra, precision=highest)  38.7 us
    dot_general x1, matrix products, filter_strip(): jnp.einsum('qkpn,hpnyxb->hqkyxb', fwd_cplx, spectra, precision=highest)  32.8 us
    dot_general x1, matrix products, filter_strip(): jnp.einsum('pkn,hzybn->hpzykb', fwd_real, box_stack, precision=highest)  30.4 us
  transfers between devices with their start and end apart: 4, of which 4 were waited for; matrix products, arithmetic and copies ran while one was open for 1% of the time, Pallas kernels for 0%

commit v1 on v0

v1 whole, which is shorter than its diff:
```python
import functools
import math

import jax
import jax.numpy as jnp
import ml_dtypes
import numpy as np
from jax import lax
from jax.experimental import pallas as pl
from jax.experimental.pallas import tpu as pltpu
from jax.sharding import PartitionSpec as P

SHELLS = 17
HALF = 17
F32 = jnp.float32
BF16 = jnp.bfloat16


def split_np(m):
    m = np.asarray(m, np.float64)
    hi = m.astype(np.float32).astype(ml_dtypes.bfloat16)
    lo = (m - hi.astype(np.float64)).astype(np.float32).astype(ml_dtypes.bfloat16)
    return hi, lo


def split(x):
    hi = x.astype(BF16)
    return hi, (x - hi.astype(F32)).astype(BF16)


def dot(a, b):
    return jnp.dot(a, b, preferred_element_type=F32)


def tables():
    n = np.arange(32)
    ang = 2.0 * np.pi / 32.0 * (n[:, None] * n[None, :] % 32)
    c, s = np.cos(ang), np.sin(ang)
    h = np.sin(np.pi * (n + 0.5) / 32.0)
    fx = np.zeros((2, 256, 2, 8, 32))
    ix = np.zeros((2, 8, 32, 2, 256))
    for b in range(8):
        v = slice(16 * b, 16 * b + 32)
        ch, sh = h[:, None] * c, h[:, None] * s
        fx[0, v, 0, b], fx[0, v, 1, b] = ch, -sh
        fx[1, v, 0, b], fx[1, v, 1, b] = sh, ch
        ix[0, b, :, 0, v], ix[0, b, :, 1, v] = ch.T, sh.T
        ix[1, b, :, 0, v], ix[1, b, :, 1, v] = -sh.T, ch.T
    fx = fx.reshape(512, 512)
    ix = ix.reshape(512, 512)
    fy = np.block([[c, s], [-s, c]]) * np.concatenate([h, h])[None, :]
    scale = 0.5 / 32768.0
    iy = np.block([[c, -s], [s, c]]) * (scale * np.concatenate([h, h]))[:, None]
    iz = np.concatenate([c[:, :17], -s[:, 1:16]], axis=1)
    iz = np.kron(iz, np.eye(8))
    out = []
    for m, axis in ((fx, 0), (fy, 1), (iy, 1), (ix, 0), (iz, 1)):
        hi, lo = split_np(m)
        out.append(np.concatenate([hi, lo, hi], axis=axis))
    return out


def z_forward(slab_slices):
    kz = jnp.arange(HALF, dtype=jnp.int32)
    step = kz[:, None] * slab_slices[None, :] % 32
    n = np.arange(32)
    table = np.stack([np.cos(2 * np.pi * n / 32), -np.sin(2 * np.pi * n / 32)])
    hi, lo = split_np(table)
    pick = (step[:, :, None] == jnp.arange(32, dtype=jnp.int32)).astype(F32)
    parts = []
    for t in (hi, lo):
        t = jnp.asarray(t.astype(np.float32))
        m = jnp.sum(pick[None] * t[:, None, None, :], axis=3).reshape(2 * HALF, 32)
        m = m[:, None, :, None] * jnp.eye(8, dtype=F32)[None, :, None, :]
        parts.append(m.reshape(2 * HALF * 8, 256).astype(BF16))
    return jnp.concatenate([parts[0], parts[1], parts[0]], axis=1)


def shell_masks(shells):
    front = shells[:HALF]
    back = jnp.roll(shells[::-1, ::-1, ::-1], (1, 1, 1), (0, 1, 2))[:HALF]
    kz = jnp.arange(HALF, dtype=jnp.int32)
    back = jnp.where(((kz > 0) & (kz < 16))[:, None, None], back, -1)
    front = front.reshape(HALF * 32, 32)
    back = back.reshape(HALF * 32, 32)
    s = jnp.arange(SHELLS, dtype=jnp.int32)

    def count(a, b, s):
        return ((a == s).astype(F32) + (b == s).astype(F32)).astype(BF16)

    wide = count(front[:, None, :], back[:, None, :], s[None, :, None])
    tall = count(front.T[None], back.T[None], s[:, None, None])
    return tall.reshape(SHELLS * 32, HALF * 32), wide.reshape(HALF * 32, SHELLS * 32)


def filter_kernel(ext, fz, fx, fy, iy, ix, iz, tall, wide, out, a_s, bhi, blo, avg, phi, plo, vox, c_s):
    for h in range(2):
        for o in range(4):
            hi, lo = split(ext[h, :, 8 * o : 8 * o + 8, :].reshape(256, 384))
            r = dot(fz[...], jnp.concatenate([hi, hi, lo], axis=0))
            a_s[h, :, 8 * o : 8 * o + 8, :] = r.reshape(2 * HALF, 8, 384)
    for h in range(2):
        for g in range(2):
            cols = slice(128 * g, 128 * g + 256)
            rhi, rlo = split(a_s[h, :HALF, :, cols].reshape(HALF * 32, 256))
            ihi, ilo = split(a_s[h, HALF:, :, cols].reshape(HALF * 32, 256))
            r = dot(jnp.concatenate([rhi, ihi, rhi, ihi, rlo, ilo], axis=1), fx[...])
            hi, lo = split(r)
            lanes = slice(256 * g, 256 * g + 256)
            bhi[h, :, :32, lanes] = hi[:, :256].reshape(HALF, 32, 256)
            bhi[h, :, 32:, lanes] = hi[:, 256:].reshape(HALF, 32, 256)
            blo[h, :, :32, lanes] = lo[:, :256].reshape(HALF, 32, 256)
            blo[h, :, 32:, lanes] = lo[:, 256:].reshape(HALF, 32, 256)

    def y_forward(kz, carry):
        spec = []
        for h in range(2):
            hi = bhi[h, kz]
            spec.append(dot(fy[...], jnp.concatenate([hi, hi, blo[h, kz]], axis=0)))
        e, o = spec
        avg[kz] = e + o
        for p, (x, y) in enumerate(((e, o), (e, e), (o, o))):
            hi, lo = split(x[:32] * y[:32] + x[32:] * y[32:])
            phi[kz, :, 512 * p : 512 * p + 512] = hi
            plo[kz, :, 512 * p : 512 * p + 512] = lo
        return carry

    lax.fori_loop(0, HALF, y_forward, 0)
    rows = SHELLS * 32
    same = lax.broadcasted_iota(jnp.int32, (32, 512), 0) == (
        lax.broadcasted_iota(jnp.int32, (32, 512), 1) % 32
    )
    group = (
        lax.broadcasted_iota(jnp.int32, (512, 512), 0) // 32
        == lax.broadcasted_iota(jnp.int32, (512, 512), 1) // 32
    ).astype(F32)
    sums = []
    for p in range(3):
        lanes = slice(512 * p, 512 * p + 512)
        t = dot(tall[...], phi[:, :, lanes].reshape(rows, 512))
        t = t + dot(tall[...], plo[:, :, lanes].reshape(rows, 512))
        t = jnp.sum(jnp.where(same[None], t.reshape(SHELLS, 32, 512), 0.0), axis=1)
        sums.append(jnp.dot(t, group, precision=lax.Precision.HIGHEST, preferred_element_type=F32))
    corr = sums[0] / jnp.sqrt(sums[1] * sums[2] + 1e-06)
    pos = jnp.maximum(corr, 0.0)
    w = 2.0 * pos / (1.0 + pos)
    w = jnp.where(same[None], w[:, None, :], 0.0).reshape(rows, 512)
    hi, lo = split(w)
    vox[...] = (dot(wide[...], hi) + dot(wide[...], lo)).reshape(HALF, 32, 512)

    def y_inverse(kz, carry):
        v = vox[kz]
        hi, lo = split(avg[kz] * jnp.concatenate([v, v], axis=0))
        r = dot(iy[...], jnp.concatenate([hi, hi, lo], axis=0))
        hi, lo = split(r)
        bhi[0, kz] = hi
        blo[0, kz] = lo
        return carry

    lax.fori_loop(0, HALF, y_inverse, 0)
    parts = []
    for g in range(2):
        lanes = slice(256 * g, 256 * g + 256)
        rhi = bhi[0, :, :32, lanes].reshape(rows, 256)
        ihi = bhi[0, :, 32:, lanes].reshape(rows, 256)
        rlo = blo[0, :, :32, lanes].reshape(rows, 256)
        ilo = blo[0, :, 32:, lanes].reshape(rows, 256)
        parts.append(dot(jnp.concatenate([rhi, ihi, rhi, ihi, rlo, ilo], axis=1), ix[...]))
    for q in range(2):
        first = parts[0][:, 256 * q : 256 * q + 256]
        second = parts[1][:, 256 * q : 256 * q + 256]
        planes = slice(HALF * q, HALF * q + HALF)
        c_s[planes, :, :128] = first[:, :128].reshape(HALF, 32, 128)
        c_s[planes, :, 128:256] = (first[:, 128:] + second[:, :128]).reshape(HALF, 32, 128)
        c_s[planes, :, 256:] = second[:, 128:].reshape(HALF, 32, 128)
    for o in range(4):
        block = slice(8 * o, 8 * o + 8)
        x = jnp.concatenate([c_s[:HALF, block, :], c_s[HALF + 1 : 2 * HALF - 1, block, :]], axis=0)
        hi, lo = split(x.reshape(256, 384))
        r = dot(iz[...], jnp.concatenate([hi, hi, lo], axis=0))
        out[:, block, :] = r.reshape(32, 8, 384)


def filter_tile(ext, slab_slices, shells):
    fx, fy, iy, ix, iz = [jnp.asarray(t) for t in tables()]
    tall, wide = shell_masks(shells)
    args = (ext, z_forward(slab_slices), fx, fy, iy, ix, iz, tall, wide)
    return pl.pallas_call(
        filter_kernel,
        out_shape=jax.ShapeDtypeStruct((32, 32, 384), F32),
        in_specs=[pl.BlockSpec(memory_space=pltpu.VMEM)] * len(args),
        out_specs=pl.BlockSpec(memory_space=pltpu.VMEM),
        scratch_shapes=[
            pltpu.VMEM((2, 2 * HALF, 32, 384), F32),
            pltpu.VMEM((2, HALF, 64, 512), BF16),
            pltpu.VMEM((2, HALF, 64, 512), BF16),
            pltpu.VMEM((HALF, 64, 512), F32),
            pltpu.VMEM((HALF, 32, 1536), BF16),
            pltpu.VMEM((HALF, 32, 1536), BF16),
            pltpu.VMEM((HALF, 32, 512), F32),
            pltpu.VMEM((2 * HALF, 32, 384), F32),
        ],
        compiler_params=pltpu.CompilerParams(vmem_limit_bytes=56 * 1024 * 1024),
    )(*args)


def from_behind(block, axis, distance):
    devices = range(lax.axis_size(axis))
    route = [(i - distance, i) for i in devices if i - distance in devices]
    return lax.ppermute(block, axis, route)


def on_device(even_half, odd_half, slab_slices, shells):
    halves_pair = jnp.stack([even_half, odd_half])
    tile_pair = lax.all_to_all(
        lax.all_to_all(halves_pair, "gy", split_axis=2, concat_axis=3, tiled=True),
        "gx",
        split_axis=3,
        concat_axis=1,
        tiled=True,
    )
    rows_tile = tile_pair.shape[2]
    cols_tile = tile_pair.shape[3]
    upper_cols = from_behind(tile_pair[:, :, :, :16], "gx", -1)
    extended = jnp.concatenate([tile_pair, upper_cols], axis=3)
    upper_rows = from_behind(extended, "gy", -1)
    extended = jnp.concatenate([extended, upper_rows], axis=2)
    extended = jnp.pad(extended, ((0, 0), (0, 0), (0, 0), (0, 112)))
    summed = filter_tile(extended, slab_slices, shells)[:, :, : cols_tile + 16]
    spill_rows = from_behind(summed[:, rows_tile:, :], "gy", 1)
    summed = jnp.concatenate([summed[:, :16, :] + spill_rows, summed[:, 16:rows_tile, :]], axis=1)
    spill_cols = from_behind(summed[:, :, cols_tile:], "gx", 1)
    filtered = jnp.concatenate([summed[:, :, :16] + spill_cols, summed[:, :, 16:cols_tile]], axis=2)
    return filtered


def solution(mesh):
    in_specs = (P("gx", None, "gy"), P("gx", None, "gy"), P(), P())
    out_specs = P(None, "gy", "gx")
    return jax.shard_map(
        on_device, mesh=mesh, in_specs=in_specs, out_specs=out_specs, check_vma=False
    )
```

time: 520 us -> 174 us (0.33); the launches traced: 510 us -> 173 us
  matrix products: 227 us -> 0 us
  local copies, waits for them, and re-layouts: 163 us -> 46.6 us
  blocking collectives: 47.1 us -> 18 us
  Pallas kernels: 0 us -> 24.9 us
  waiting for transfers between devices: 41.2 us -> 49 us
  starting transfers between devices: 11.3 us -> 17.8 us
    dot_general x9 -> x0, matrix products: 227 us -> none  [the longest x1 58.1 us: filter_strip(): jnp.einsum('qkpn,hpznxb->hqzkxb', fwd_cplx, spectra, precision=highest)]
    transpose x3 -> x2, local copies, waits for them, and re-layouts: 86.1 us -> 0.27 us  [shell_masks(): tall = count(front.T[None], back.T[None], s[:, None, None])]
    all_to_all x1 -> x0, blocking collectives: 29.1 us -> none  [on_device(): lax.all_to_all(lax.all_to_all(halves_pair, 'gy', split_axis=2, concat_axi...]
    pallas_call x0 -> x1, Pallas kernels: none -> 24.9 us  [filter_tile(): pl.pallas_call(filter_kernel, out_shape=jax.ShapeDtypeStruct((32, 32, 384...]
    all_to_all x0 -> x1, waiting for transfers between devices: none -> 22 us  [on_device(): lax.all_to_all(lax.all_to_all(halves_pair, 'gy', split_axis=2, concat_axi...]
    reshape x1 -> x2, local copies, waits for them, and re-layouts: 20.9 us -> 0.27 us  [the longest x1 0.14 us: shell_masks(): front = front.reshape(HALF * 32, 32)]
    mul x2, local copies, waits for them, and re-layouts: 14.3 us -> 0.01 us  [z_forward(): m = m[:, None, :, None] * jnp.eye(8, dtype=F32)[None, :, None, :]]
    ppermute x4, waiting for transfers between devices: 41.2 us -> 27.1 us  [from_behind(): return lax.ppermute(block, axis, route)]
  transfers between devices with their start and end apart: 4 -> 5, of which waited for: 4 -> 4; matrix products, arithmetic and copies ran while one was open for 1% -> 15% of each run, Pallas kernels for 0% -> 0%
where the time goes in v1:
time: 174 us; the launch traced here: 173 us
  waiting for transfers between devices  49 us (28%)
  local copies, waits for them, and re-layouts  46.6 us (27%)
  Pallas kernels  24.9 us (14%)
  blocking collectives  18 us (10%)
  starting transfers between devices  17.8 us (10%)
  other arithmetic  16.4 us (9%)
    ppermute x4, waiting for transfers between devices, from_behind(): return lax.ppermute(block, axis, route)  27.1 us
    pallas_call x1, Pallas kernels, filter_tile(): pl.pallas_call(filter_kernel, out_shape=jax.ShapeDtypeStruct((32, 32, 384...  24.9 us
    all_to_all x1, waiting for transfers between devices, on_device(): lax.all_to_all(lax.all_to_all(halves_pair, 'gy', split_axis=2, concat_axi...  22 us
    all_to_all x1, blocking collectives, on_device(): lax.all_to_all(halves_pair, 'gy', split_axis=2, concat_axis=3, tiled=True)  18 us
    unnamed x20, local copies, waits for them, and re-layouts  12.6 us
    ppermute x4, starting transfers between devices, from_behind(): return lax.ppermute(block, axis, route)  12.4 us
    convert_element_type x2, local copies, waits for them, and re-layouts, z_forward(): parts.append(m.reshape(2 * HALF * 8, 256).astype(BF16))  8.36 us
    eq x6, local copies, waits for them, and re-layouts, count(): return ((a == s).astype(F32) + (b == s).astype(F32)).astype(BF16)  7.3 us
  transfers between devices with their start and end apart: 5, of which 4 were waited for; matrix products, arithmetic and copies ran while one was open for 15% of the time, Pallas kernels for 0%

profile of v1, /device:TPU:10, one launch (start us, length us, event | category | flops | bytes accessed | tf_op | source)
XLA Modules:
  0.0 173.0 jit_solution(16972136189337942954)
XLA Ops:
  0.0 1.8 %copy_bitcast_fusion = (f32[1,8,128,128]{3,1,0,2:T(8,128)S(1)}, f32[1,8,128,128]{3,1,0,2:T(8,128)S(1)}) fusion(f32[8,128,128]{2,1,0:T(8,128)} %param.12, f32[8,128,128]{2,1,0:T(8,128)} %param.11), kind=kLoop, calls=%fused_computation.18 | loop fusion | bytes 2097152 | tf_op jit(solution)/shard_map/stack | solution.py:214
  1.9 18.0 %all_to_all.36 = f32[2,8,128,128]{3,1,0,2:T(8,128)S(1)} all-to-all(f32[2,8,128,128]{3,1,0,2:T(8,128)S(1)} %pad_maximum_fusion.1), channel_id=1, replica_groups=mesh['gy'=8,'gx'=4] {'gy'}, dimensions={2} | all-to-all | bytes 2097152 | tf_op jit(solution)/shard_map/all_to_all | solution.py:216
  19.8 5.0 %copy.46 = f32[2,8,16,8,128]{2,1,0,4,3:T(8,128)} copy(f32[2,8,16,8,128]{4,1,0,2,3:T(8,128)S(1)} %bitcast.41) | data formatting | bytes 2097152 | tf_op jit(solution)/shard_map/all_to_all | solution.py:216
  24.8 6.4 %reshape.84 = f32[4,1,65536]{2,1,0:T(1,128)} reshape(f32[1024,2,8,16]{3,2,1,0:T(8,128)} %bitcast.34) | data formatting | bytes 2097152
  31.2 5.5 %all-to-all-start.1 = ((f32[4,1,65536]{2,1,0:T(1,128)}), f32[4,1,65536]{2,1,0:T(1,128)S(1)}, u32[]{:S(2)}, u32[]{:S(2)}) async-start(f32[4,1,65536]{2,1,0:T(1,128)} %reshape.84), calls=%async_computation.1 | async-start | bytes 2097152 | tf_op jit(solution)/shard_map/all_to_all | solution.py:215
  36.7 0.1 fusion.1
  36.9 0.4 multiply_reduce_fusion
  37.3 22.0 %all-to-all-done.1 = f32[4,1,65536]{2,1,0:T(1,128)S(1)} async-done(((f32[4,1,65536]{2,1,0:T(1,128)}), f32[4,1,65536]{2,1,0:T(1,128)S(1)}, u32[]{:S(2)}, u32[]{:S(2)}) %all-to-all-start.1) | async-done | bytes 1048608 | tf_op jit(solution)/shard_map/all_to_all | solution.py:215
  59.2 0.5 broadcast.90
  59.7 3.7 %reduce = f32[4,65536]{1,0:T(4,128)S(1)} reduce(f32[4,1,65536]{2,1,0:T(1,128)S(1)} %all-to-all-done.1, f32[]{:T(128)} %broadcast.90), dimensions={1}, to_apply=%all_to_all.30.reduce_sub_computation | reduce | bytes 2097156 | tf_op jit(solution)/shard_map/all_to_all | solution.py:215
  63.4 6.1 %reshape.85 = f32[1024,2,8,16]{3,2,1,0:T(8,128)} reshape(f32[4,65536]{1,0:T(4,128)S(1)} %reduce) | data formatting | bytes 2097152
  69.6 5.3 %copy.47 = f32[2,8,16,4,256]{4,3,2,1,0:T(4,128)S(1)} copy(f32[2,8,16,4,256]{2,1,0,4,3:T(8,128)} %bitcast.35) | data formatting | bytes 2097152 | tf_op jit(solution)/shard_map/all_to_all | solution.py:215
  74.9 0.2 copy.39
  75.1 5.2 %collective-permute-start = (f32[2,32,16,16]{3,2,1,0:T(8,128)S(1)}, f32[2,32,16,16]{3,2,1,0:T(8,128)S(1)}, u32[]{:S(2)}, u32[]{:S(2)}) collective-permute-start(f32[2,32,16,16]{3,2,1,0:T(8,128)S(1)} %slice.73), channel_id=1, source_target_pairs={{1,0},{2,1},{3,2},{5,4},{6,5},{7,6},{9,8},{10,9},{11,10},{13,12},{... | collective-permute-start | bytes 196616 | tf_op jit(solution)/shard_map/ppermute | solution.py:210
  80.3 10.4 %collective-permute-done = f32[2,32,16,16]{3,2,1,0:T(8,128)S(1)} collective-permute-done((f32[2,32,16,16]{3,2,1,0:T(8,128)S(1)}, f32[2,32,16,16]{3,2,1,0:T(8,128)S(1)}, u32[]{:S(2)}, u32[]{:S(2)}) %collective-permute-start) | collective-permute-done | bytes 65568 | tf_op jit(solution)/shard_map/ppermute | solution.py:210
  90.7 1.3 pad_maximum_fusion
  92.1 2.2 %collective-permute-start.1 = (f32[2,32,16,272]{3,2,1,0:T(8,128)}, f32[2,32,16,272]{3,2,1,0:T(8,128)}, u32[]{:S(2)}, u32[]{:S(2)}) collective-permute-start(f32[2,32,16,272]{3,2,1,0:T(8,128)} %pad_maximum_fusion), channel_id=1, source_target_pairs={{4,0},{8,4},{12,8},{16,12},{20,16},{24,20},{28,24},{5,1},{9,5},{13... | collective-permute-start | bytes 3342344 | tf_op jit(solution)/shard_map/ppermute | solution.py:210
  94.3 2.1 %multiply_convert_fusion = (bf16[34,8,32,8]{3,2,1,0:T(8,128)(2,1)S(1)}, bf16[34,8,32,8]{3,2,1,0:T(8,128)(2,1)}) fusion(f32[34,32]{1,0:T(8,128)S(1)} %mul.87, f32[8,8]{1,0:T(8,128)S(1)} %fusion.6, f32[34,32]{1,0:T(8,128)S(1)} %mul.81), kind=kLoop, calls=%fused_computation | loop fusion | flops 278528 | bytes 287488 | tf_op jit(solution)/shard_map/convert_element_type | solution.py:75
  96.4 0.8 slice.61
  97.3 0.6 slice.59
  97.9 4.8 %convert_element_type.58 = bf16[272,256]{1,0:T(8,128)(2,1)} reshape(bf16[34,8,32,8]{3,2,1,0:T(8,128)(2,1)} %get-tuple-element.10) | data formatting | bytes 278528 | tf_op jit(solution)/shard_map/convert_element_type | solution.py:75
  102.6 3.6 %convert_element_type.60 = bf16[272,256]{1,0:T(8,128)(2,1)} reshape(bf16[34,8,32,8]{3,2,1,0:T(8,128)(2,1)S(1)} %get-tuple-element.9) | data formatting | bytes 278528 | tf_op jit(solution)/shard_map/convert_element_type | solution.py:75
  106.2 1.2 slice.62
  107.5 0.8 slice.60
  108.4 0.1 pad_add_fusion
  108.4 0.2 slice_add_fusion.1
  108.7 0.2 fusion
  108.8 0.1 copy.44
  109.0 1.3 eq.126
  110.2 1.8 %copy.45 = s32[544,544]{1,0:T(8,128)S(1)} copy(s32[544,544]{0,1:T(8,128)} %bitcast.39) | data formatting | bytes 2367488 | tf_op jit(solution)/shard_map/eq | solution.py:89
  112.0 0.1 copy.42
  112.2 1.2 eq.122
  113.4 2.9 %copy.43 = s32[544,544]{1,0:T(8,128)} copy(s32[544,544]{0,1:T(8,128)} %bitcast.40) | data formatting | bytes 2367488 | tf_op jit(solution)/shard_map/eq | solution.py:89
  116.3 0.1 eq.116
  116.4 0.1 copy.41
  116.5 0.1 copy.40
  116.7 2.9 %add_convert_fusion = (bf16[544,544]{1,0:T(8,128)(2,1)}, bf16[544,544]{1,0:T(8,128)(2,1)}) fusion(s32[544,544]{1,0:T(8,128)S(1)} %copy.45, s32[544,544]{1,0:T(8,128)} %copy.43, s32[544]{0:T(1024)S(1)} %eq.116, s32[32,544]{1,0:T(8,128)S(1)} %copy.41, s32[32,544]{1,0:T(8,128)S(1)} %copy.40), kind=kLoop, calls=%fused_computation.8 | loop fusion | flops 3551232 | bytes 3692672 | tf_op jit(solution)/shard_map/convert_element_type | solution.py:89
  119.6 0.8 pad_maximum_fusion.3.fz
  120.4 3.3 %select_maximum_fusion.ext = f32[2,32,32,384]{3,2,1,0:T(8,128)} fusion(f32[2,32,16,272]{3,2,1,0:T(8,128)} %collective-permute-done.1, f32[2,32,16,16]{3,2,1,0:T(8,128)S(1)} %copy-done.2, f32[2,32,16,256]{3,2,1,0:T(8,128)S(1)} %bitcast.38), kind=kLoop, calls=%fused_computation.2 | loop fusion | flops 4718592 | bytes 5373952 | tf_op jit(solution)/shard_map/concatenate | solution.py:227
  123.7 24.9 %shard_map.109 = f32[32,32,384]{2,1,0:T(8,128)} custom-call(f32[2,32,32,384]{3,2,1,0:T(8,128)} %select_maximum_fusion.ext, bf16[272,768]{1,0:T(8,128)(2,1)} %pad_maximum_fusion.3.fz, bf16[1536,512]{1,0:T(8,128)(2,1)} %constant.38.clone.fx, bf16[64,192]{1,0:T(8,128)(2,1)} %constant.39.clone.fy, bf16[64,192]{1,0:T(8,128)(2,1)} %constant.40.clone.iy, ...), custom_call_target="tpu_custom_call" | custom-call | tf_op jit(solution)/shard_map/pallas_call | solution.py:188
  148.6 1.3 slice.77
  149.9 2.4 %collective-permute-start.2 = (f32[32,16,272]{2,1,0:T(8,128)S(1)}, f32[32,16,272]{2,1,0:T(8,128)S(1)}, u32[]{:S(2)}, u32[]{:S(2)}) collective-permute-start(f32[32,16,272]{2,1,0:T(8,128)S(1)} %slice.77), channel_id=1, source_target_pairs={{0,4},{4,8},{8,12},{12,16},{16,20},{20,24},{24,28},{1,5},{5,9},{9,... | collective-permute-start | bytes 1671176 | tf_op jit(solution)/shard_map/ppermute | solution.py:210
  152.3 10.9 %collective-permute-done.2 = f32[32,16,272]{2,1,0:T(8,128)S(1)} collective-permute-done((f32[32,16,272]{2,1,0:T(8,128)S(1)}, f32[32,16,272]{2,1,0:T(8,128)S(1)}, u32[]{:S(2)}, u32[]{:S(2)}) %collective-permute-start.2) | collective-permute-done | bytes 557088 | tf_op jit(solution)/shard_map/ppermute | solution.py:210
  163.2 0.1 slice_add_fusion
  163.4 2.6 %collective-permute-start.3 = (f32[32,16,16]{2,1,0:T(8,128)S(1)}, f32[32,16,16]{2,1,0:T(8,128)S(1)}, u32[]{:S(2)}, u32[]{:S(2)}) collective-permute-start(f32[32,16,16]{2,1,0:T(8,128)S(1)} %slice.79), channel_id=1, source_target_pairs={{0,1},{1,2},{2,3},{4,5},{5,6},{6,7},{8,9},{9,10},{10,11},{12,13},{... | collective-permute-start | bytes 98312 | tf_op jit(solution)/shard_map/ppermute | solution.py:210
  166.0 0.2 slice.80
  166.2 5.8 %collective-permute-done.3 = f32[32,16,16]{2,1,0:T(8,128)S(1)} collective-permute-done((f32[32,16,16]{2,1,0:T(8,128)S(1)}, f32[32,16,16]{2,1,0:T(8,128)S(1)}, u32[]{:S(2)}, u32[]{:S(2)}) %collective-permute-start.3) | collective-permute-done | bytes 32800 | tf_op jit(solution)/shard_map/ppermute | solution.py:210
  172.0 1.0 pad_maximum_fusion.2
  (32 shorter events, 0.3 us)
Async XLA Ops:
  31.2 5.5 %copy-start.8 = (s32[32]{0:T(128)S(1)}, s32[32]{0:T(128)}, u32[]{:S(2)}) copy-start(s32[32]{0:T(128)} %param.13) | copy-start | bytes 388
  31.2 5.6 %copy-start.6 = (f32[2,32]{1,0:T(2,128)S(1)}, f32[2,32]{1,0:T(2,128)}, u32[]{:S(2)}) copy-start(f32[2,32]{1,0:T(2,128)} %constant.44.clone) | copy-start | bytes 772
  31.2 5.6 %copy-start.7 = (f32[2,32]{1,0:T(2,128)S(1)}, f32[2,32]{1,0:T(2,128)}, u32[]{:S(2)}) copy-start(f32[2,32]{1,0:T(2,128)} %constant.43.clone) | copy-start | bytes 772
  31.2 28.0 %all-to-all-start.1 = ((f32[4,1,65536]{2,1,0:T(1,128)}), f32[4,1,65536]{2,1,0:T(1,128)S(1)}, u32[]{:S(2)}, u32[]{:S(2)}) async-start(f32[4,1,65536]{2,1,0:T(1,128)} %reshape.84), calls=%async_computation.1 | async-start | bytes 2097152 | tf_op jit(solution)/shard_map/all_to_all | solution.py:215
  75.1 15.6 %collective-permute-start = (f32[2,32,16,16]{3,2,1,0:T(8,128)S(1)}, f32[2,32,16,16]{3,2,1,0:T(8,128)S(1)}, u32[]{:S(2)}, u32[]{:S(2)}) collective-permute-start(f32[2,32,16,16]{3,2,1,0:T(8,128)S(1)} %slice.73), channel_id=1, source_target_pairs={{1,0},{2,1},{3,2},{5,4},{6,5},{7,6},{9,8},{10,9},{11,10},{13,12},{... | collective-permute-start | bytes 196616 | tf_op jit(solution)/shard_map/ppermute | solution.py:210
  90.7 1.3 copy-start.1
  92.1 4.4 %copy-start.3 = (s32[32,32,32]{2,1,0:T(8,128)S(1)}, s32[32,32,32]{2,1,0:T(8,128)}, u32[]{:S(2)}) copy-start(s32[32,32,32]{2,1,0:T(8,128)} %param.14) | copy-start | bytes 393220
  92.1 28.3 %collective-permute-start.1 = (f32[2,32,16,272]{3,2,1,0:T(8,128)}, f32[2,32,16,272]{3,2,1,0:T(8,128)}, u32[]{:S(2)}, u32[]{:S(2)}) collective-permute-start(f32[2,32,16,272]{3,2,1,0:T(8,128)} %pad_maximum_fusion), channel_id=1, source_target_pairs={{4,0},{8,4},{12,8},{16,12},{20,16},{24,20},{28,24},{5,1},{9,5},{13... | collective-permute-start | bytes 3342344 | tf_op jit(solution)/shard_map/ppermute | solution.py:210
  116.7 2.9 %copy-start.4 = (bf16[272,256]{1,0:T(8,128)(2,1)S(1)}, bf16[272,256]{1,0:T(8,128)(2,1)}, u32[]{:S(2)}) copy-start(bf16[272,256]{1,0:T(8,128)(2,1)} %convert_element_type.58) | copy-start | bytes 417796
  116.7 2.9 %copy-start.5 = (bf16[272,256]{1,0:T(8,128)(2,1)S(1)}, bf16[272,256]{1,0:T(8,128)(2,1)}, u32[]{:S(2)}) copy-start(bf16[272,256]{1,0:T(8,128)(2,1)} %convert_element_type.60) | copy-start | bytes 417796
  116.7 3.7 %copy-start.2 = (f32[2,32,16,16]{3,2,1,0:T(8,128)S(1)}, f32[2,32,16,16]{3,2,1,0:T(8,128)}, u32[]{:S(2)}) copy-start(f32[2,32,16,16]{3,2,1,0:T(8,128)} %copy-done.1) | copy-start | bytes 196612
  148.6 14.6 %copy-start = (f32[32,32,384]{2,1,0:T(8,128)S(1)}, f32[32,32,384]{2,1,0:T(8,128)}, u32[]{:S(2)}) copy-start(f32[32,32,384]{2,1,0:T(8,128)} %shard_map.109) | copy-start | bytes 4718596
  149.9 13.3 %collective-permute-start.2 = (f32[32,16,272]{2,1,0:T(8,128)S(1)}, f32[32,16,272]{2,1,0:T(8,128)S(1)}, u32[]{:S(2)}, u32[]{:S(2)}) collective-permute-start(f32[32,16,272]{2,1,0:T(8,128)S(1)} %slice.77), channel_id=1, source_target_pairs={{0,4},{4,8},{8,12},{12,16},{16,20},{20,24},{24,28},{1,5},{5,9},{9,... | collective-permute-start | bytes 1671176 | tf_op jit(solution)/shard_map/ppermute | solution.py:210
  163.4 8.6 %collective-permute-start.3 = (f32[32,16,16]{2,1,0:T(8,128)S(1)}, f32[32,16,16]{2,1,0:T(8,128)S(1)}, u32[]{:S(2)}, u32[]{:S(2)}) collective-permute-start(f32[32,16,16]{2,1,0:T(8,128)S(1)} %slice.79), channel_id=1, source_target_pairs={{0,1},{1,2},{2,3},{4,5},{5,6},{6,7},{8,9},{9,10},{10,11},{12,13},{... | collective-permute-start | bytes 98312 | tf_op jit(solution)/shard_map/ppermute | solution.py:210

commit v2 on v1

--- a/solution.py
+++ b/solution.py
@@ -1,5 +1,4 @@
 import functools
-import math
 
 import jax
 import jax.numpy as jnp
@@ -60,44 +59,58 @@
     return out
 
 
-def z_forward(slab_slices):
-    kz = jnp.arange(HALF, dtype=jnp.int32)
-    step = kz[:, None] * slab_slices[None, :] % 32
-    n = np.arange(32)
-    table = np.stack([np.cos(2 * np.pi * n / 32), -np.sin(2 * np.pi * n / 32)])
-    hi, lo = split_np(table)
-    pick = (step[:, :, None] == jnp.arange(32, dtype=jnp.int32)).astype(F32)
-    parts = []
-    for t in (hi, lo):
-        t = jnp.asarray(t.astype(np.float32))
-        m = jnp.sum(pick[None] * t[:, None, None, :], axis=3).reshape(2 * HALF, 32)
-        m = m[:, None, :, None] * jnp.eye(8, dtype=F32)[None, :, None, :]
-        parts.append(m.reshape(2 * HALF * 8, 256).astype(BF16))
-    return jnp.concatenate([parts[0], parts[1], parts[0]], axis=1)
-
-
-def shell_masks(shells):
+def shell_pair(shells):
     front = shells[:HALF]
     back = jnp.roll(shells[::-1, ::-1, ::-1], (1, 1, 1), (0, 1, 2))[:HALF]
     kz = jnp.arange(HALF, dtype=jnp.int32)
     back = jnp.where(((kz > 0) & (kz < 16))[:, None, None], back, -1)
-    front = front.reshape(HALF * 32, 32)
-    back = back.reshape(HALF * 32, 32)
-    s = jnp.arange(SHELLS, dtype=jnp.int32)
-
-    def count(a, b, s):
-        return ((a == s).astype(F32) + (b == s).astype(F32)).astype(BF16)
-
-    wide = count(front[:, None, :], back[:, None, :], s[None, :, None])
-    tall = count(front.T[None], back.T[None], s[:, None, None])
-    return tall.reshape(SHELLS * 32, HALF * 32), wide.reshape(HALF * 32, SHELLS * 32)
-
-
-def filter_kernel(ext, fz, fx, fy, iy, ix, iz, tall, wide, out, a_s, bhi, blo, avg, phi, plo, vox, c_s):
+    pair = jnp.stack([front.reshape(HALF * 32, 32), back.reshape(HALF * 32, 32)])
+    return jnp.tile(pair, (1, 1, 4)), jnp.transpose(pair, (0, 2, 1))
+
+
+def head_lanes(x, k):
+    lane = lax.broadcasted_iota(jnp.int32, x.shape, 1)
+    return jnp.where(lane < 16, pltpu.roll(x, (128 - 16 * k) % 128, 1) if k else x, 0.0)
+
+
+def place_lanes(x, k):
+    lane = lax.broadcasted_iota(jnp.int32, x.shape, 1)
+    x = jnp.where(lane < 16, x, 0.0)
+    return pltpu.roll(x, 16 * k, 1) if k else x
+
+
+def filter_kernel(
+    main, packed, slab, pairs, turned, zt, fx, fy, iy, ix, iz, out, tail_out,
+    rim, tall, wide, a_s, bhi, blo, avg, phi, plo, vox, c_s,
+):
+    for i in range(5):
+        shell = 4 * i + lax.broadcasted_iota(jnp.int32, (HALF * 32, 128), 1) // 32
+        m = (pairs[0] == shell).astype(F32) + (pairs[1] == shell).astype(F32)
+        wide[:, 128 * i : 128 * i + 128] = m.astype(BF16)
+    for s in range(SHELLS):
+        m = (turned[0] == s).astype(F32) + (turned[1] == s).astype(F32)
+        tall[32 * s : 32 * s + 32, :] = m.astype(BF16)
+    place = lax.broadcasted_iota(jnp.int32, (256, 256), 0)
+    place = (place // 8 == slab[...]) & (
+        place % 8 == lax.broadcasted_iota(jnp.int32, (256, 256), 1) % 8
+    )
+    place = place.astype(F32).astype(BF16)
+    zhi = dot(zt[0], place).astype(BF16)
+    zlo = dot(zt[1], place).astype(BF16)
+    fz = jnp.concatenate([zhi, zlo, zhi], axis=1)
+    slots = 32 // packed.shape[0]
+    for s in range(packed.shape[0]):
+        for h in range(2):
+            for k in range(slots):
+                rim[h, slots * s + k] = head_lanes(packed[s, h], k)
     for h in range(2):
         for o in range(4):
-            hi, lo = split(ext[h, :, 8 * o : 8 * o + 8, :].reshape(256, 384))
-            r = dot(fz[...], jnp.concatenate([hi, hi, lo], axis=0))
+            block = slice(8 * o, 8 * o + 8)
+            x = jnp.concatenate(
+                [main[0, h, :, block, :], main[1, h, :, block, :], rim[h, :, block, :]], axis=2
+            )
+            hi, lo = split(x.reshape(256, 384))
+            r = dot(fz, jnp.concatenate([hi, hi, lo], axis=0))
             a_s[h, :, 8 * o : 8 * o + 8, :] = r.reshape(2 * HALF, 8, 384)
     for h in range(2):
         for g in range(2):
@@ -145,6 +158,7 @@
     pos = jnp.maximum(corr, 0.0)
     w = 2.0 * pos / (1.0 + pos)
     w = jnp.where(same[None], w[:, None, :], 0.0).reshape(rows, 512)
+    w = jnp.concatenate([w, jnp.zeros((640 - rows, 512), F32)], axis=0)
     hi, lo = split(w)
     vox[...] = (dot(wide[...], hi) + dot(wide[...], lo)).reshape(HALF, 32, 512)
 
@@ -178,19 +192,39 @@
         x = jnp.concatenate([c_s[:HALF, block, :], c_s[HALF + 1 : 2 * HALF - 1, block, :]], axis=0)
         hi, lo = split(x.reshape(256, 384))
         r = dot(iz[...], jnp.concatenate([hi, hi, lo], axis=0))
-        out[:, block, :] = r.reshape(32, 8, 384)
-
-
-def filter_tile(ext, slab_slices, shells):
-    fx, fy, iy, ix, iz = [jnp.asarray(t) for t in tables()]
-    tall, wide = shell_masks(shells)
-    args = (ext, z_forward(slab_slices), fx, fy, iy, ix, iz, tall, wide)
+        r = r.reshape(32, 8, 384)
+        out[0, :, block, :] = r[:, :, :128]
+        out[1, :, block, :] = r[:, :, 128:256]
+        rim[0, :, block, :] = r[:, :, 256:]
+    for q in range(4):
+        tail_out[q] = sum(place_lanes(rim[0, 8 * q + k], k) for k in range(8))
+
+
+def z_table():
+    n = np.arange(32)
+    ang = 2.0 * np.pi / 32.0 * (n[:, None] * n[None, :] % 32)
+    m = np.concatenate([np.cos(ang)[:HALF], -np.sin(ang)[:HALF]], axis=0)
+    return np.stack(split_np(np.kron(m, np.eye(8))))
+
+
+def filter_tile(main, packed, slab_slices, shells):
+    consts = [jnp.asarray(t) for t in tables()]
+    pairs, turned = shell_pair(shells)
+    slab = jnp.repeat(slab_slices, 8).reshape(1, 256)
+    args = (main, packed, slab, pairs, turned, jnp.asarray(z_table()), *consts)
+    vmem = pl.BlockSpec(memory_space=pltpu.VMEM)
     return pl.pallas_call(
         filter_kernel,
-        out_shape=jax.ShapeDtypeStruct((32, 32, 384), F32),
-        in_specs=[pl.BlockSpec(memory_space=pltpu.VMEM)] * len(args),
-        out_specs=pl.BlockSpec(memory_space=pltpu.VMEM),
+        out_shape=(
+            jax.ShapeDtypeStruct((2, 32, 32, 128), F32),
+            jax.ShapeDtypeStruct((4, 32, 128), F32),
+        ),
+        in_specs=[vmem] * len(args),
+        out_specs=(vmem, vmem),
         scratch_shapes=[
+            pltpu.VMEM((2, 32, 32, 128), F32),
+            pltpu.VMEM((SHELLS * 32, HALF * 32), BF16),
+            pltpu.VMEM((HALF * 32, 640), BF16),
             pltpu.VMEM((2, 2 * HALF, 32, 384), F32),
             pltpu.VMEM((2, HALF, 64, 512), BF16),
             pltpu.VMEM((2, HALF, 64, 512), BF16),
@@ -204,34 +238,290 @@
     )(*args)
 
 
-def from_behind(block, axis, distance):
-    devices = range(lax.axis_size(axis))
-    route = [(i - distance, i) for i in devices if i - distance in devices]
-    return lax.ppermute(block, axis, route)
+def remote(src, dst, send, recv, device):
+    return pltpu.make_async_remote_copy(
+        src_ref=src, dst_ref=dst, send_sem=send, recv_sem=recv,
+        device_id=device, device_id_type=pl.DeviceIdType.MESH,
+    )
+
+
+def gather_kernel(
+    G, N, even, odd, main, packed, stage, pack,
+    send_a, recv_a, send_b, recv_b, send_h, recv_h, send_c, recv_c, send_d, recv_d,
+):
+    slots = 32 // N
+    per = G // N
+    g, s = lax.axis_index("gy"), lax.axis_index("gx")
+    barrier = pltpu.get_barrier_semaphore()
+    for i in range(1, G):
+        pl.semaphore_signal(
+            barrier, inc=1, device_id=(lax.rem(g + i, G), s), device_id_type=pl.DeviceIdType.MESH
+        )
+    for i in range(1, N):
+        pl.semaphore_signal(
+            barrier, inc=1, device_id=(g, lax.rem(s + i, N)), device_id_type=pl.DeviceIdType.MESH
+        )
+    pl.semaphore_wait(barrier, G + N - 2)
+
+    def rows_of(k):
+        return pl.ds(pl.multiple_of(16 * k, 16), 16)
+
+    def copy_a(i, h):
+        to = lax.rem(g + i, G)
+        src = (even, odd)[h]
+        return remote(
+            src.at[:, rows_of(to), :], stage.at[i, h], send_a.at[i, h], recv_a.at[i, h], (to, s)
+        )
+
+    for i in range(1, G):
+        for h in range(2):
+            copy_a(i, h).start()
+    stage[0, 0] = even[:, rows_of(g), :]
+    stage[0, 1] = odd[:, rows_of(g), :]
+
+    def source(i):
+        g0 = lax.rem(g + G - i, G)
+        return g0 // per, lax.rem(g0, per)
+
+    def part(t, z, r):
+        return main.at[t, :, pl.ds(slots * z, slots), pl.ds(r, 16), :]
+
+    def copy_b(i):
+        c, t = source(i)
+        return remote(stage.at[i], part(t, s, 0), send_b.at[i], recv_b.at[s, t], (g, c))
+
+    def local_b(i):
+        t = source(i)[1]
+        return pltpu.make_async_copy(stage.at[i], part(t, s, 0), send_b.at[i])
+
+    def copy_h(i):
+        c = source(i)[0] - 1
+        return remote(
+            pack.at[i], packed.at[s, :, pl.ds(0, 16), :], send_h.at[i], recv_h.at[s], (g, c)
+        )
+
+    for i in range(G):
+        if i:
+            for h in range(2):
+                copy_a(i, h).wait_recv()
+        c, t = source(i)
+
+        @pl.when(c == s)
+        def _():
+            local_b(i).start()
+
+        @pl.when(c != s)
+        def _():
+            copy_b(i).start()
+
+        @pl.when((t == 0) & (c > 0))
+        def _():
+            for h in range(2):
+                pack[i, h] = sum(place_lanes(stage[i, h, k], k) for k in range(slots))
+
+        @pl.when((t == 0) & (c > 0) & (c != s + 1))
+        def _():
+            copy_h(i).start()
+
+        @pl.when((t == 0) & (c > 0) & (c == s + 1))
+        def _():
+            packed[s, :, 0:16, :] = pack[i]
+
+    for i in range(G):
+
+        @pl.when(source(i)[0] == s)
+        def _():
+            local_b(i).wait()
+
+    def copy_c(j, t):
+        z = lax.rem(s + j, N)
+        return remote(part(t, z, 0), part(t, z, 16), send_c.at[j, t], recv_c.at[j, t], (g - 1, s))
+
+    def wait_b(j, t):
+        z = lax.rem(s + j, N)
+        remote(part(t, z, 0), part(t, z, 0), send_c.at[j, t], recv_b.at[z, t], (g, z)).wait_recv()
+
+    order = [0] + [k for d in range(1, N) for k in (d, N - d)]
+    order = list(dict.fromkeys(order))
+    for j in order:
+        for t in range(per):
+            if j:
+                wait_b(j, t)
+
+            @pl.when(g > 0)
+            def _():
+                copy_c(j, t).start()
+
+    @pl.when(s < N - 1)
+    def _():
+        for j in range(1, N):
+            z = lax.rem(s + j, N)
+            block = packed.at[z, :, pl.ds(0, 16), :]
+            remote(block, block, send_d.at[0], recv_h.at[z], (g, z)).wait_recv()
+
+    @pl.when(s == N - 1)
+    def _():
+        packed[:, :, 0:16, :] = jnp.zeros((N, 2, 16, 128), F32)
+
+    def copy_d():
+        return remote(
+            packed.at[:, :, pl.ds(0, 16), :], packed.at[:, :, pl.ds(16, 16), :],
+            send_d.at[0], recv_d.at[0], (g - 1, s),
+        )
+
+    @pl.when(g > 0)
+    def _():
+        copy_d().start()
+
+    @pl.when(g == G - 1)
+    def _():
+        packed[:, :, 16:32, :] = jnp.zeros((N, 2, 16, 128), F32)
+        main[:, :, :, 16:32, :] = jnp.zeros((per, 2, 32, 16, 128), F32)
+
+    @pl.when(g < G - 1)
+    def _():
+        for j in order:
+            for t in range(per):
+                copy_c(j, t).wait_recv()
+        copy_d().wait_recv()
+
+    for i in range(1, G):
+        for h in range(2):
+            copy_a(i, h).wait_send()
+    for i in range(G):
+        c, t = source(i)
+
+        @pl.when(c != s)
+        def _():
+            copy_b(i).wait_send()
+
+        @pl.when((t == 0) & (c > 0) & (c != s + 1))
+        def _():
+            copy_h(i).wait_send()
+
+    @pl.when(g > 0)
+    def _():
+        for j in order:
+            for t in range(per):
+                copy_c(j, t).wait_send()
+        copy_d().wait_send()
+
+
+def gather(even, odd):
+    G, N = lax.axis_size("gy"), lax.axis_size("gx")
+    slots, per = 32 // N, G // N
+    vmem = pl.BlockSpec(memory_space=pltpu.VMEM)
+    dma = pltpu.SemaphoreType.DMA
+    return pl.pallas_call(
+        functools.partial(gather_kernel, G, N),
+        out_shape=(
+            jax.ShapeDtypeStruct((per, 2, 32, 32, 128), F32),
+            jax.ShapeDtypeStruct((N, 2, 32, 128), F32),
+        ),
+        in_specs=[vmem, vmem],
+        out_specs=(vmem, vmem),
+        scratch_shapes=[
+            pltpu.VMEM((G, 2, slots, 16, 128), F32),
+            pltpu.VMEM((G, 2, 16, 128), F32),
+            dma((G, 2)), dma((G, 2)), dma((G,)), dma((N, per)), dma((G,)), dma((N,)),
+            dma((N, per)), dma((N, per)), dma((1,)), dma((1,)),
+        ],
+        compiler_params=pltpu.CompilerParams(
+            collective_id=0, has_side_effects=True, vmem_limit_bytes=32 * 1024 * 1024
+        ),
+    )(even, odd)
+
+
+def spill_kernel(G, N, body, tail, out, rows, top, low, send, recv):
+    g, s = lax.axis_index("gy"), lax.axis_index("gx")
+    barrier = pltpu.get_barrier_semaphore()
+    steps = ((1, 0), (0, 1), (1, 1))
+
+    def ahead(dg, ds):
+        return (g < G - dg) & (s < N - ds)
+
+    def behind(dg, ds):
+        return (g >= dg) & (s >= ds)
+
+    for dg, ds in steps:
+
+        @pl.when(ahead(dg, ds))
+        def _():
+            pl.semaphore_signal(
+                barrier, inc=1, device_id=(g + dg, s + ds), device_id_type=pl.DeviceIdType.MESH
+            )
+
+        @pl.when(behind(dg, ds))
+        def _():
+            pl.semaphore_signal(
+                barrier, inc=1, device_id=(g - dg, s - ds), device_id_type=pl.DeviceIdType.MESH
+            )
+
+    peers = sum(f(*d).astype(jnp.int32) for f in (ahead, behind) for d in steps)
+    pl.semaphore_wait(barrier, peers)
+
+    sources = (
+        body.at[:, :, pl.ds(16, 16), :], tail.at[:, pl.ds(0, 16), :], tail.at[:, pl.ds(16, 16), :]
+    )
+    targets = (rows, top, low)
+
+    def copy(k):
+        dg, ds = steps[k]
+        return remote(sources[k], targets[k], send.at[k], recv.at[k], (g + dg, s + ds))
+
+    for k in range(3):
+
+        @pl.when(ahead(*steps[k]))
+        def _():
+            copy(k).start()
+
+        @pl.when(jnp.logical_not(behind(*steps[k])))
+        def _():
+            targets[k][...] = jnp.zeros(targets[k].shape, F32)
+
+    for k in range(3):
+
+        @pl.when(behind(*steps[k]))
+        def _():
+            copy(k).wait_recv()
+
+    for z in range(32):
+        q = z // 8
+        rim = head_lanes(top[q] + low[q], z % 8)
+        out[z, :, :128] = body[0, z, :16, :] + rows[0, z] + rim
+        out[z, :, 128:] = body[1, z, :16, :] + rows[1, z]
+    for k in range(3):
+
+        @pl.when(ahead(*steps[k]))
+        def _():
+            copy(k).wait_send()
+
+
+def spill(body, tail):
+    G, N = lax.axis_size("gy"), lax.axis_size("gx")
+    vmem = pl.BlockSpec(memory_space=pltpu.VMEM)
+    dma = pltpu.SemaphoreType.DMA
+    return pl.pallas_call(
+        functools.partial(spill_kernel, G, N),
+        out_shape=jax.ShapeDtypeStruct((32, 16, 256), F32),
+        in_specs=[vmem, vmem],
+        out_specs=vmem,
+        scratch_shapes=[
+            pltpu.VMEM((2, 32, 16, 128), F32),
+            pltpu.VMEM((4, 16, 128), F32),
+            pltpu.VMEM((4, 16, 128), F32),
+            dma((3,)), dma((3,)),
+        ],
+        compiler_params=pltpu.CompilerParams(
+            collective_id=1, has_side_effects=True, vmem_limit_bytes=32 * 1024 * 1024
+        ),
+    )(body, tail)
 
 
 def on_device(even_half, odd_half, slab_slices, shells):
-    halves_pair = jnp.stack([even_half, odd_half])
-    tile_pair = lax.all_to_all(
-        lax.all_to_all(halves_pair, "gy", split_axis=2, concat_axis=3, tiled=True),
-        "gx",
-        split_axis=3,
-        concat_axis=1,
-        tiled=True,
-    )
-    rows_tile = tile_pair.shape[2]
-    cols_tile = tile_pair.shape[3]
-    upper_cols = from_behind(tile_pair[:, :, :, :16], "gx", -1)
-    extended = jnp.concatenate([tile_pair, upper_cols], axis=3)
-    upper_rows = from_behind(extended, "gy", -1)
-    extended = jnp.concatenate([extended, upper_rows], axis=2)
-    extended = jnp.pad(extended, ((0, 0), (0, 0), (0, 0), (0, 112)))
-    summed = filter_tile(extended, slab_slices, shells)[:, :, : cols_tile + 16]
-    spill_rows = from_behind(summed[:, rows_tile:, :], "gy", 1)
-    summed = jnp.concatenate([summed[:, :16, :] + spill_rows, summed[:, 16:rows_tile, :]], axis=1)
-    spill_cols = from_behind(summed[:, :, cols_tile:], "gx", 1)
-    filtered = jnp.concatenate([summed[:, :, :16] + spill_cols, summed[:, :, 16:cols_tile]], axis=2)
-    return filtered
+    main, packed = gather(even_half, odd_half)
+    body, tail = filter_tile(main, packed, slab_slices, shells)
+    return spill(body, tail)
 
 
 def solution(mesh):

time: 174 us -> 86.3 us (0.50)
  Pallas kernels: 24.9 us -> 75 us
  waiting for transfers between devices: 49 us -> 0 us
  local copies, waits for them, and re-layouts: 46.6 us -> 9.64 us
  blocking collectives: 18 us -> 0 us
  starting transfers between devices: 17.8 us -> 0 us
  other arithmetic: 16.4 us -> 1.25 us
    pallas_call x1 -> x3, Pallas kernels: 24.9 us -> 75 us  [the longest x1 37.5 us: gather(): pl.pallas_call(functools.partial(gather_kernel, G, N), out_shape=(jax.Sha...]
    ppermute x4 -> x0, waiting for transfers between devices: 27.1 us -> none  [from_behind(): return lax.ppermute(block, axis, route)]
    all_to_all x1 -> x0, waiting for transfers between devices: 22 us -> none  [on_device(): lax.all_to_all(lax.all_to_all(halves_pair, 'gy', split_axis=2, concat_axi...]
    all_to_all x1 -> x0, blocking collectives: 18 us -> none  [on_device(): lax.all_to_all(halves_pair, 'gy', split_axis=2, concat_axis=3, tiled=True)]
    ppermute x4 -> x0, starting transfers between devices: 12.4 us -> none  [from_behind(): return lax.ppermute(block, axis, route)]
    all_to_all x4 -> x0, local copies, waits for them, and re-layouts: 11 us -> none  [the longest x3 5.99 us: on_device(): lax.all_to_all(lax.all_to_all(halves_pair, 'gy', split_axis=2, concat_axi...]
    convert_element_type x2 -> x0, local copies, waits for them, and re-layouts: 8.36 us -> none  [z_forward(): parts.append(m.reshape(2 * HALF * 8, 256).astype(BF16))]
    unnamed x20 -> x13, local copies, waits for them, and re-layouts: 12.6 us -> 4.84 us
  transfers between devices with their start and end apart: 5 -> 0, of which waited for: 4 -> 0; matrix products, arithmetic and copies ran while one was open for 15% -> 0% of each run, Pallas kernels for 0% -> 0%
where the time goes in v2:
time: 86.3 us; the launch traced here: 86 us
  Pallas kernels  75 us (87%)
  local copies, waits for them, and re-layouts  9.64 us (11%)
  other arithmetic  1.25 us (1%)
    pallas_call x1, Pallas kernels, gather(): pl.pallas_call(functools.partial(gather_kernel, G, N), out_shape=(jax.Sha...  37.5 us
    pallas_call x1, Pallas kernels, filter_tile(): pl.pallas_call(filter_kernel, out_shape=(jax.ShapeDtypeStruct((2, 32, 32,...  25.1 us
    pallas_call x1, Pallas kernels, spill(): pl.pallas_call(functools.partial(spill_kernel, G, N), out_shape=jax.Shape...  12.5 us
    unnamed x13, local copies, waits for them, and re-layouts  4.84 us

profile of v2, /device:TPU:10, one launch (start us, length us, event | category | flops | bytes accessed | tf_op | source)
XLA Modules:
  0.0 86.0 jit_solution(8839527583901662912)
XLA Ops:
  0.0 0.0 slice-start
  0.0 0.8 broadcast_in_dim.16
  0.8 0.7 reshape_reshape.3.slab
  1.5 0.7 slice.37
  2.2 0.1 slice.38
  2.3 1.0 %slice.36 = s32[17,32,32]{2,1,0:T(8,128)S(1)} slice(s32[32,32,32]{2,1,0:T(8,128)} %param.13), slice={[0:17], [0:32], [0:32]} | slice | bytes 139264 | tf_op jit(solution)/shard_map/slice | solution.py:63
  3.2 0.1 copy.17
  3.4 0.0 slice-done
  3.4 0.2 slice.40
  3.7 0.1 pad_add_fusion
  3.7 0.2 slice_add_fusion
  4.0 0.2 fusion
  4.2 0.0 copy-start.2
  4.2 0.0 copy-start.3
  4.2 0.1 copy.18
  4.3 0.7 fusion.1
  5.1 1.1 %copy.16.pairs = s32[2,544,128]{2,1,0:T(8,128)} copy(s32[2,544,128]{1,2,0:T(8,128)S(1)} %bitcast.5) | data formatting | bytes 1114112 | tf_op jit(solution)/shard_map/tile | solution.py:68
  6.1 0.0 copy-done.2
  6.1 0.0 copy-done.3
  6.1 37.5 %shard_map.100 = (f32[2,2,32,32,128]{4,3,2,1,0:T(8,128)S(1)}, f32[4,2,32,128]{3,2,1,0:T(8,128)S(1)}) custom-call(f32[8,128,128]{2,1,0:T(8,128)S(1)} %copy-done.2, f32[8,128,128]{2,1,0:T(8,128)S(1)} %copy-done.3), custom_call_target="tpu_custom_call" | custom-call | tf_op jit(solution)/shard_map/pallas_call | solution.py:415
  43.6 0.0 copy-start
  43.6 1.3 %copy-done = f32[2,2,32,32,128]{4,3,2,1,0:T(8,128)} copy-done((f32[2,2,32,32,128]{4,3,2,1,0:T(8,128)}, f32[2,2,32,32,128]{4,3,2,1,0:T(8,128)S(1)}, u32[]{:S(2)}) %copy-start) | copy-done | bytes 2097176
  45.0 0.0 copy-start.4
  45.0 0.6 copy-done.4
  45.6 25.1 %shard_map.101 = (f32[2,32,32,128]{3,2,1,0:T(8,128)}, f32[4,32,128]{2,1,0:T(8,128)}) custom-call(f32[2,2,32,32,128]{4,3,2,1,0:T(8,128)} %copy-done, f32[4,2,32,128]{3,2,1,0:T(8,128)} %copy-done.4, s32[1,256]{1,0:T(1,128)} %reshape_reshape.3.slab, s32[2,544,128]{2,1,0:T(8,128)} %copy.16.pairs, s32[2,32,544]{2,1,0:T(8,128)} %get-tuple-element.13.turned, ...), custom_call_target="tpu_custom_call" | custom-call | tf_op jit(solution)/shard_map/pallas_call | solution.py:216
  70.7 0.0 copy-start.1
  70.7 1.2 %copy-done.1 = f32[2,32,32,128]{3,2,1,0:T(8,128)S(1)} copy-done((f32[2,32,32,128]{3,2,1,0:T(8,128)S(1)}, f32[2,32,32,128]{3,2,1,0:T(8,128)}, u32[]{:S(2)}) %copy-start.1) | copy-done | bytes 1048600
  71.9 0.0 copy-start.5
  71.9 0.8 copy-done.5
  72.7 12.5 %shard_map.102 = f32[32,16,256]{2,1,0:T(8,128)S(1)} custom-call(f32[2,32,32,128]{3,2,1,0:T(8,128)S(1)} %copy-done.1, f32[4,32,128]{2,1,0:T(8,128)S(1)} %copy-done.5), custom_call_target="tpu_custom_call" | custom-call | tf_op jit(solution)/shard_map/pallas_call | solution.py:504
  85.2 0.8 copy.20
  (4 shorter events, 0.1 us)
Async XLA Ops:
  0.0 3.4 %slice-start = ((s32[32,32,32]{2,1,0:T(8,128)}), s32[31,32,32]{2,1,0:T(8,128)S(1)}, s32[]{:S(2)}) async-start(s32[32,32,32]{2,1,0:T(8,128)} %param.13), calls=%async_computation | async-start | bytes 1015808 | tf_op jit(solution)/shard_map/jit(_roll_static)/slice | solution.py:64
  4.2 2.0 %copy-start.2 = (f32[8,128,128]{2,1,0:T(8,128)S(1)}, f32[8,128,128]{2,1,0:T(8,128)}, u32[]{:S(2)}) copy-start(f32[8,128,128]{2,1,0:T(8,128)} %even.1) | copy-start | bytes 1572868
  4.2 2.0 %copy-start.3 = (f32[8,128,128]{2,1,0:T(8,128)S(1)}, f32[8,128,128]{2,1,0:T(8,128)}, u32[]{:S(2)}) copy-start(f32[8,128,128]{2,1,0:T(8,128)} %odd.1) | copy-start | bytes 1572868
  43.6 1.3 %copy-start = (f32[2,2,32,32,128]{4,3,2,1,0:T(8,128)}, f32[2,2,32,32,128]{4,3,2,1,0:T(8,128)S(1)}, u32[]{:S(2)}) copy-start(f32[2,2,32,32,128]{4,3,2,1,0:T(8,128)S(1)} %get-tuple-element.9.main) | copy-start | bytes 6291460
  45.0 0.6 copy-start.4
  70.7 1.2 %copy-start.1 = (f32[2,32,32,128]{3,2,1,0:T(8,128)S(1)}, f32[2,32,32,128]{3,2,1,0:T(8,128)}, u32[]{:S(2)}) copy-start(f32[2,32,32,128]{3,2,1,0:T(8,128)} %get-tuple-element.11.body) | copy-start | bytes 3145732
  71.9 0.8 copy-start.5

commit v3 on v2

--- a/solution.py
+++ b/solution.py
@@ -59,15 +59,6 @@
     return out
 
 
-def shell_pair(shells):
-    front = shells[:HALF]
-    back = jnp.roll(shells[::-1, ::-1, ::-1], (1, 1, 1), (0, 1, 2))[:HALF]
-    kz = jnp.arange(HALF, dtype=jnp.int32)
-    back = jnp.where(((kz > 0) & (kz < 16))[:, None, None], back, -1)
-    pair = jnp.stack([front.reshape(HALF * 32, 32), back.reshape(HALF * 32, 32)])
-    return jnp.tile(pair, (1, 1, 4)), jnp.transpose(pair, (0, 2, 1))
-
-
 def head_lanes(x, k):
     lane = lax.broadcasted_iota(jnp.int32, x.shape, 1)
     return jnp.where(lane < 16, pltpu.roll(x, (128 - 16 * k) % 128, 1) if k else x, 0.0)
@@ -80,21 +71,44 @@
 
 
 def filter_kernel(
-    main, packed, slab, pairs, turned, zt, fx, fy, iy, ix, iz, out, tail_out,
+    main, packed, slab, shells, zt, fx, fy, iy, ix, iz, out, tail_out,
     rim, tall, wide, a_s, bhi, blo, avg, phi, plo, vox, c_s,
 ):
+    def iota(shape, axis):
+        return lax.broadcasted_iota(jnp.int32, shape, axis)
+
+    def exact(mask):
+        return mask.astype(F32).astype(BF16)
+
+    numbers = shells[...].astype(F32).astype(BF16)
+    tile = exact(iota((32, 128), 1) % 32 == iota((32, 128), 0))
+    tile_back = exact((32 - iota((32, 128), 1) % 32) % 32 == iota((32, 128), 0))
+    turn = exact(iota((32, 32), 0) == iota((32, 32), 1))
+    turn_back = exact((32 - iota((32, 32), 0)) % 32 == iota((32, 32), 1))
+    front = dot(numbers[: HALF * 32], tile)
+    flipped = dot(numbers, tile_back).astype(BF16)
+    none = jnp.full((32, 128), -1.0, F32)
+    back = [none] + [dot(turn_back, flipped[32 * (32 - k) : 32 * (33 - k)]) for k in range(1, 16)]
+    back = jnp.concatenate(back + [none], axis=0)
+    sides = (((1,), (1,)), ((), ()))
+    front_t = lax.dot_general(
+        turn, front[:, :32].astype(BF16), sides, preferred_element_type=F32
+    )
+    back_t = lax.dot_general(turn, back[:, :32].astype(BF16), sides, preferred_element_type=F32)
     for i in range(5):
-        shell = 4 * i + lax.broadcasted_iota(jnp.int32, (HALF * 32, 128), 1) // 32
-        m = (pairs[0] == shell).astype(F32) + (pairs[1] == shell).astype(F32)
+        shell = (4 * i + iota((HALF * 32, 128), 1) // 32).astype(F32)
+        m = (front == shell).astype(F32) + (back == shell).astype(F32)
         wide[:, 128 * i : 128 * i + 128] = m.astype(BF16)
     for s in range(SHELLS):
-        m = (turned[0] == s).astype(F32) + (turned[1] == s).astype(F32)
+        m = (front_t == s).astype(F32) + (back_t == s).astype(F32)
         tall[32 * s : 32 * s + 32, :] = m.astype(BF16)
-    place = lax.broadcasted_iota(jnp.int32, (256, 256), 0)
-    place = (place // 8 == slab[...]) & (
-        place % 8 == lax.broadcasted_iota(jnp.int32, (256, 256), 1) % 8
+    spread = exact(iota((32, 256), 1) // 8 == iota((32, 256), 0))
+    slices = jnp.broadcast_to(slab[...].astype(F32), (8, 32)).astype(BF16)
+    slices = dot(slices, spread)[0:1]
+    place = iota((256, 256), 0)
+    place = exact(
+        ((place // 8).astype(F32) == slices) & (place % 8 == iota((256, 256), 1) % 8)
     )
-    place = place.astype(F32).astype(BF16)
     zhi = dot(zt[0], place).astype(BF16)
     zlo = dot(zt[1], place).astype(BF16)
     fz = jnp.concatenate([zhi, zlo, zhi], axis=1)
@@ -209,9 +223,7 @@
 
 def filter_tile(main, packed, slab_slices, shells):
     consts = [jnp.asarray(t) for t in tables()]
-    pairs, turned = shell_pair(shells)
-    slab = jnp.repeat(slab_slices, 8).reshape(1, 256)
-    args = (main, packed, slab, pairs, turned, jnp.asarray(z_table()), *consts)
+    args = (main, packed, slab_slices.reshape(1, 32), shells.reshape(1024, 32), jnp.asarray(z_table()), *consts)
     vmem = pl.BlockSpec(memory_space=pltpu.VMEM)
     return pl.pallas_call(
         filter_kernel,
@@ -234,7 +246,7 @@
             pltpu.VMEM((HALF, 32, 512), F32),
             pltpu.VMEM((2 * HALF, 32, 384), F32),
         ],
-        compiler_params=pltpu.CompilerParams(vmem_limit_bytes=56 * 1024 * 1024),
+        compiler_params=pltpu.CompilerParams(vmem_limit_bytes=44 * 1024 * 1024),
     )(*args)
 
 
@@ -427,7 +439,7 @@
             dma((N, per)), dma((N, per)), dma((1,)), dma((1,)),
         ],
         compiler_params=pltpu.CompilerParams(
-            collective_id=0, has_side_effects=True, vmem_limit_bytes=32 * 1024 * 1024
+            collective_id=0, has_side_effects=True, vmem_limit_bytes=12 * 1024 * 1024
         ),
     )(even, odd)
 
@@ -513,7 +525,7 @@
             dma((3,)), dma((3,)),
         ],
         compiler_params=pltpu.CompilerParams(
-            collective_id=1, has_side_effects=True, vmem_limit_bytes=32 * 1024 * 1024
+            collective_id=1, has_side_effects=True, vmem_limit_bytes=12 * 1024 * 1024
         ),
     )(body, tail)
 

time: 86.3 us -> 82.8 us (0.959)
  Pallas kernels: 75 us -> 71.3 us
  local copies, waits for them, and re-layouts: 9.64 us -> 10.9 us
  other arithmetic: 1.25 us -> 0 us
    unnamed x13 -> x21, local copies, waits for them, and re-layouts: 4.84 us -> 10.9 us
    pallas_call x1, Pallas kernels: 25.1 us -> 21.3 us  [filter_tile(): pl.pallas_call(filter_kernel, out_shape=(jax.ShapeDtypeStruct((2, 32, 32,...]
    another operation x5 -> x0, local copies, waits for them, and re-layouts: 2.03 us -> none  [the longest x2 1.1 us: shell_pair(): return (jnp.tile(pair, (1, 1, 4)), jnp.transpose(pair, (0, 2, 1)))]
    slice x6 -> x0, local copies, waits for them, and re-layouts: 1.99 us -> none  [the longest x5 1.01 us: shell_pair(): back = jnp.roll(shells[::-1, ::-1, ::-1], (1, 1, 1), (0, 1, 2))[:HALF]]
where the time goes in v3:
time: 82.8 us; the launch traced here: 82.2 us
  Pallas kernels  71.3 us (86%)
  local copies, waits for them, and re-layouts  10.9 us (13%)
    pallas_call x1, Pallas kernels, gather(): pl.pallas_call(functools.partial(gather_kernel, G, N), out_shape=(jax.Sha...  37.5 us
    pallas_call x1, Pallas kernels, filter_tile(): pl.pallas_call(filter_kernel, out_shape=(jax.ShapeDtypeStruct((2, 32, 32,...  21.3 us
    pallas_call x1, Pallas kernels, spill(): pl.pallas_call(functools.partial(spill_kernel, G, N), out_shape=jax.Shape...  12.5 us
    unnamed x21, local copies, waits for them, and re-layouts  10.9 us

profile of v3, /device:TPU:10, one launch (start us, length us, event | category | flops | bytes accessed | tf_op | source)
XLA Modules:
  0.0 82.2 jit_solution(9760094770611779388)
XLA Ops:
  0.0 0.0 copy-start.2
  0.0 1.0 %copy-done.2 = f32[8,128,128]{2,1,0:T(8,128)S(1)} copy-done((f32[8,128,128]{2,1,0:T(8,128)S(1)}, f32[8,128,128]{2,1,0:T(8,128)}, u32[]{:S(2)}) %copy-start.2) | copy-done | bytes 524312
  1.0 0.0 copy-start.3
  1.0 1.0 %copy-done.3 = f32[8,128,128]{2,1,0:T(8,128)S(1)} copy-done((f32[8,128,128]{2,1,0:T(8,128)S(1)}, f32[8,128,128]{2,1,0:T(8,128)}, u32[]{:S(2)}) %copy-start.3) | copy-done | bytes 524312
  2.1 37.5 %shard_map.100 = (f32[2,2,32,32,128]{4,3,2,1,0:T(8,128)S(1)}, f32[4,2,32,128]{3,2,1,0:T(8,128)S(1)}) custom-call(f32[8,128,128]{2,1,0:T(8,128)S(1)} %copy-done.2, f32[8,128,128]{2,1,0:T(8,128)S(1)} %copy-done.3), custom_call_target="tpu_custom_call" | custom-call | tf_op jit(solution)/shard_map/pallas_call | solution.py:427
  39.6 0.0 copy-start
  39.6 1.4 %copy-done = bf16[1536,512]{1,0:T(8,128)(2,1)S(1)} copy-done((bf16[1536,512]{1,0:T(8,128)(2,1)S(1)}, bf16[1536,512]{1,0:T(8,128)(2,1)}, u32[]{:S(2)}) %copy-start) | copy-done | bytes 1572888
  41.0 0.0 copy-start.1
  41.0 1.4 %copy-done.1 = bf16[1536,512]{1,0:T(8,128)(2,1)S(1)} copy-done((bf16[1536,512]{1,0:T(8,128)(2,1)S(1)}, bf16[1536,512]{1,0:T(8,128)(2,1)}, u32[]{:S(2)}) %copy-start.1) | copy-done | bytes 1572888
  42.4 0.0 copy-start.4
  42.4 1.0 %copy-done.4 = s32[32,32,32]{2,1,0:T(8,128)S(1)} copy-done((s32[32,32,32]{2,1,0:T(8,128)S(1)}, s32[32,32,32]{2,1,0:T(8,128)}, u32[]{:S(2)}) %copy-start.4) | copy-done | bytes 131096
  43.5 0.0 copy-start.5
  43.5 1.0 %copy-done.5 = bf16[256,768]{1,0:T(8,128)(2,1)S(1)} copy-done((bf16[256,768]{1,0:T(8,128)(2,1)S(1)}, bf16[256,768]{1,0:T(8,128)(2,1)}, u32[]{:S(2)}) %copy-start.5) | copy-done | bytes 393240
  44.4 0.0 copy-start.6
  44.4 1.0 %copy-done.6 = bf16[2,272,256]{2,1,0:T(8,128)(2,1)S(1)} copy-done((bf16[2,272,256]{2,1,0:T(8,128)(2,1)S(1)}, bf16[2,272,256]{2,1,0:T(8,128)(2,1)}, u32[]{:S(2)}) %copy-start.6) | copy-done | bytes 278552
  45.4 0.0 copy-start.7
  45.4 0.8 copy-done.7
  46.2 0.0 copy-start.8
  46.2 0.8 copy-done.8
  46.9 0.0 copy-start.9
  46.9 0.7 copy-done.9
  47.6 21.3 %shard_map.101 = (f32[2,32,32,128]{3,2,1,0:T(8,128)S(1)}, f32[4,32,128]{2,1,0:T(8,128)S(1)}) custom-call(f32[2,2,32,32,128]{4,3,2,1,0:T(8,128)S(1)} %get-tuple-element.9.main, f32[4,2,32,128]{3,2,1,0:T(8,128)S(1)} %get-tuple-element.10.packed, s32[1,32]{1,0:T(1,128)S(1)} %bitcast.3, s32[1024,32]{1,0:T(8,128)S(1)} %bitcast.2, ...), custom_call_target="tpu_custom_call" | custom-call | tf_op jit(solution)/shard_map/pallas_call | solution.py:228
  68.9 12.5 %shard_map.102 = f32[32,16,256]{2,1,0:T(8,128)S(1)} custom-call(f32[2,32,32,128]{3,2,1,0:T(8,128)S(1)} %get-tuple-element.11.body, f32[4,32,128]{2,1,0:T(8,128)S(1)} %get-tuple-element.12.tail), custom_call_target="tpu_custom_call" | custom-call | tf_op jit(solution)/shard_map/pallas_call | solution.py:516
  81.4 0.8 copy.12
Async XLA Ops:
  0.0 1.0 %copy-start.2 = (f32[8,128,128]{2,1,0:T(8,128)S(1)}, f32[8,128,128]{2,1,0:T(8,128)}, u32[]{:S(2)}) copy-start(f32[8,128,128]{2,1,0:T(8,128)} %even.1) | copy-start | bytes 1572868
  1.0 1.0 %copy-start.3 = (f32[8,128,128]{2,1,0:T(8,128)S(1)}, f32[8,128,128]{2,1,0:T(8,128)}, u32[]{:S(2)}) copy-start(f32[8,128,128]{2,1,0:T(8,128)} %odd.1) | copy-start | bytes 1572868
  39.6 1.4 %copy-start = (bf16[1536,512]{1,0:T(8,128)(2,1)S(1)}, bf16[1536,512]{1,0:T(8,128)(2,1)}, u32[]{:S(2)}) copy-start(bf16[1536,512]{1,0:T(8,128)(2,1)} %constant.15.clone.ix) | copy-start | bytes 4718596
  41.0 1.4 %copy-start.1 = (bf16[1536,512]{1,0:T(8,128)(2,1)S(1)}, bf16[1536,512]{1,0:T(8,128)(2,1)}, u32[]{:S(2)}) copy-start(bf16[1536,512]{1,0:T(8,128)(2,1)} %constant.12.clone.fx) | copy-start | bytes 4718596
  42.4 1.0 %copy-start.4 = (s32[32,32,32]{2,1,0:T(8,128)S(1)}, s32[32,32,32]{2,1,0:T(8,128)}, u32[]{:S(2)}) copy-start(s32[32,32,32]{2,1,0:T(8,128)} %param.13) | copy-start | bytes 393220
  43.5 1.0 %copy-start.5 = (bf16[256,768]{1,0:T(8,128)(2,1)S(1)}, bf16[256,768]{1,0:T(8,128)(2,1)}, u32[]{:S(2)}) copy-start(bf16[256,768]{1,0:T(8,128)(2,1)} %constant.16.clone.iz) | copy-start | bytes 1179652
  44.4 1.0 %copy-start.6 = (bf16[2,272,256]{2,1,0:T(8,128)(2,1)S(1)}, bf16[2,272,256]{2,1,0:T(8,128)(2,1)}, u32[]{:S(2)}) copy-start(bf16[2,272,256]{2,1,0:T(8,128)(2,1)} %constant.17.clone.zt) | copy-start | bytes 835588
  45.4 0.8 copy-start.7
  46.2 0.8 copy-start.8
  46.9 0.7 copy-start.9
